TPU v7x, 32 devices: a whole 2x2x4 slice. The times are simulated.
32 devices in a mesh: half: 2 (over x), panel: 4 (over y, core), dom: 4 (over z).
Axes of the slice: x: 2, y: 2, z: 4, core: 2. Of those that a mesh axis runs over, the one named last changes fastest.
Arguments:
- images: bfloat16 [512, 8192], P(('half', 'dom')), parts along dimension 0, may hold values from -128 to 128
- shift_index: int32 [512, 9], P(('half', 'dom')), parts along dimension 0, may hold values from 0 to 48, as said below
- references: bfloat16 [128, 8192], P(('half', 'panel', 'dom')), parts along dimension 0, may hold values from -0.6 to 0.6
- slot_blocks: int32 [128, 8], P(('half', 'panel')), parts along dimension 0, may hold values from 0 to 31
Outputs:
- volume: float32 [64, 1024], P(('half', 'panel', 'dom')), parts along dimension 0
- log_evidence: float32 [512], P(('half', 'dom')), parts along dimension 0
There are 2 independent parts, one for each index of `half`. A program takes and returns all parts, laid end to end along the dimension named above; each array names one. Nothing has to cross between parts.
Inputs may be any that keep to these rules, and one draw needn't show every extreme that they name: `shift_index`: each row names 9 different offsets.
All inputs are finite; a program needn't handle non-finite values.
Results may differ from a plain program's by a relative error of at most 0.0048.
Values may be sent and summed in bfloat16 or wider, within the bound.
A program may use at most 128 MiB of HBM per device.

v0:
```python
import math

import jax
import jax.numpy as jnp
from jax import lax
from jax.sharding import PartitionSpec as P

PIX = 64
SHIFTS = 9
GRID = 7
VB_DEV = 2


offset_sigma = 2.0


def offsets(shift_index):
    shift_row = (shift_index // GRID - GRID // 2).astype(jnp.float32)
    shift_col = (shift_index % GRID - GRID // 2).astype(jnp.float32)
    return (shift_row, shift_col)


def penalty(shift_index):
    shift_row, shift_col = offsets(shift_index)
    return (shift_row * shift_row + shift_col * shift_col) * (0.5 / (offset_sigma * offset_sigma))


def phase_table():
    shift_row, shift_col = offsets(jnp.arange(GRID * GRID, dtype=jnp.int32))
    frequency = jnp.arange(PIX, dtype=jnp.float32) - PIX // 2
    phase_angle = (
        -2.0
        * math.pi
        / PIX
        * (
            shift_row[:, None, None] * frequency[None, :, None]
            + shift_col[:, None, None] * frequency[None, None, :]
        )
    )
    return (jnp.cos(phase_angle), jnp.sin(phase_angle))


def shift_images(images, shift_index, cos_table, sin_table):
    row_count = images.shape[0]
    cosine = cos_table[shift_index]
    sine_part = sin_table[shift_index]
    picture = images.astype(jnp.float32).reshape(row_count, 1, PIX, 2, PIX)
    real_part = picture[:, :, :, 0, :]
    imag_part = picture[:, :, :, 1, :]
    out_real = real_part * cosine - imag_part * sine_part
    out_imag = real_part * sine_part + imag_part * cosine
    return (
        jnp.stack([out_real, out_imag], axis=3)
        .reshape(row_count * SHIFTS, 2 * PIX * PIX)
        .astype(jnp.bfloat16)
    )


def score_rows(images, shift_index, gathered, block_size):
    cos_table, sin_table = phase_table()
    row_count = images.shape[0]
    block_count = row_count // block_size
    ref_norms = jnp.sum(jnp.square(gathered.astype(jnp.float32)), axis=1)
    image_blocks = images.reshape(block_count, block_size, images.shape[1])
    index_blocks = shift_index.reshape(block_count, block_size, SHIFTS)

    def one_block(blocks):
        image_block, index_block = blocks
        moved = shift_images(image_block, index_block, cos_table, sin_table)
        correlation = lax.dot_general(
            moved, gathered, (((1,), (1,)), ((), ())), preferred_element_type=jnp.float32
        )
        return (correlation - 0.5 * ref_norms[None, :] - penalty(index_block).reshape(-1, 1), moved)

    scores, moved_blocks = lax.map(one_block, (image_blocks, index_blocks))
    return (scores.reshape(row_count, SHIFTS * gathered.shape[0]), moved_blocks)


def back_project(moved_blocks, weights, slot_table, group_count, block_total):
    block_count = moved_blocks.shape[0]
    block_rows = moved_blocks.shape[1]
    row_width = moved_blocks.shape[2]
    orient_count = slot_table.shape[0]
    segments = slot_table.shape[1]
    block_len = row_width // segments
    group_rows = orient_count // group_count
    weight_blocks = weights.reshape(block_count, block_rows, orient_count)

    def one_group(group_index, volume):

        def add_block(running, inputs):
            moved, weight_block = inputs
            return (
                running
                + lax.dot_general(
                    weight_block,
                    moved,
                    (((0,), (0,)), ((), ())),
                    preferred_element_type=jnp.float32,
                ),
                None,
            )

        slab_sums, _ = lax.scan(
            add_block,
            jnp.zeros((group_rows, row_width), jnp.float32),
            (moved_blocks, weight_blocks),
        )
        return volume.at[slot_table.reshape(-1)].add(
            slab_sums.reshape(group_rows * segments, block_len)
        )

    return lax.fori_loop(
        0, group_count, one_group, jnp.zeros((block_total, block_len), jnp.float32)
    )


def shards(images, shift_index, references, slot_blocks):
    n_panel = lax.axis_size("panel")
    n_dom = lax.axis_size("dom")
    part_dev = images.shape[0]
    segments = slot_blocks.shape[1]
    block_total = VB_DEV * n_panel * n_dom
    volume_scale = (part_dev * n_dom * segments / block_total) ** (-0.5)
    gathered = lax.all_gather(references, "dom", axis=0, tiled=True)
    block_size = min(64, part_dev)
    scores, moved_blocks = score_rows(images, shift_index, gathered, block_size)
    row_top = lax.pmax(jnp.max(scores, axis=1), "panel")
    raised = jnp.exp(scores - row_top[:, None])
    row_total = lax.psum(jnp.sum(raised, axis=1), "panel")
    weights = (raised / row_total[:, None]).astype(jnp.bfloat16)
    log_evidence = row_top + jnp.log(row_total)
    partial_value = back_project(moved_blocks, weights, slot_blocks, 1, block_total)
    summed = lax.psum_scatter(partial_value, ("panel", "dom"), scatter_dimension=0, tiled=True)
    return (summed * volume_scale, log_evidence)


def solution(mesh):
    in_specs = (
        P(("half", "dom"), None),
        P(("half", "dom"), None),
        P(("half", "panel", "dom"), None),
        P(("half", "panel"), None),
    )
    out_specs = (P(("half", "panel", "dom"), None), P(("half", "dom")))
    return jax.shard_map(shards, mesh=mesh, in_specs=in_specs, out_specs=out_specs, check_vma=False)
```

profile of v0, /device:TPU:0, one launch (start us, length us, event | category | flops | bytes accessed | tf_op | source)
XLA Modules:
  0.0 251.5 jit_solution(21198172485179252)
XLA Ops:
  7.2 0.7 compare_select_fusion
  7.9 0.7 fusion.13
  9.0 5.7 %fusion = (f32[49,64,64]{2,1,0:T(8,128)S(1)}, f32[49,64,64]{2,1,0:T(8,128)S(1)}) fusion(f32[49,64]{1,0:T(8,128)S(1)} %get-tuple-element.62, f32[49,64]{1,0:T(8,128)S(1)} %get-tuple-element.52), kind=kLoop, calls=%fused_computation.7 | loop fusion | flops 401408 | bytes 1630720 | tf_op jit(solution)/shard_map/sin | solution.py:40
  14.7 7.9 %gather_fusion = f32[576,64,64]{2,1,0:T(8,128)} fusion(f32[49,64,64]{2,1,0:T(8,128)S(1)} %get-tuple-element.51, s32[1024]{0:T(1024)S(1)} %pad_clamp_fusion), kind=kCustom, calls=%fused_computation | custom fusion | bytes 18876672 | tf_op jit(solution)/shard_map/while/body/eval_jaxpr/gather | solution.py:45
  22.6 7.7 %gather_fusion.1 = f32[576,64,64]{2,1,0:T(8,128)} fusion(f32[49,64,64]{2,1,0:T(8,128)S(1)} %get-tuple-element.50, s32[1024]{0:T(1024)S(1)} %pad_clamp_fusion), kind=kCustom, calls=%fused_computation.1 | custom fusion | bytes 18876672 | tf_op jit(solution)/shard_map/while/body/eval_jaxpr/gather | solution.py:46
  30.3 4.4 %reshape.214 = f32[64,1,64,2,64]{4,3,2,0,1:T(2,128)} reshape(bf16[64,8192]{1,0:T(8,128)(2,1)S(1)} %copy-done) | data formatting | bytes 3145728 | tf_op jit(solution)/shard_map/while/body/eval_jaxpr/convert_element_type | solution.py:47
  34.8 7.9 %fusion.23 = (f32[64,1,64,1,64]{4,3,2,0,1:T(1,128)S(1)}, f32[64,1,64,1,64]{4,3,2,0,1:T(1,128)S(1)}) fusion(f32[64,1,64,2,64]{4,3,2,0,1:T(2,128)} %reshape.214), kind=kLoop, calls=%fused_computation.52 | loop fusion | bytes 4194304 | tf_op jit(solution)/shard_map/while/body/eval_jaxpr/slice | solution.py:48
  42.6 17.8 %subtract_convert_fusion = (bf16[64,9,64,1,64]{4,2,3,1,0:T(8,128)(2,1)S(1)}, bf16[64,9,64,1,64]{4,2,3,1,0:T(8,128)(2,1)}) fusion(f32[64,9,64,1,64]{4,2,3,1,0:T(8,128)} %bitcast.16, f32[64,9,64,1,64]{4,2,3,1,0:T(8,128)} %bitcast.15, f32[64,64,64]{2,1,0:T(8,128)S(1)} %bitcast.18, f32[64,64,64]{2,1,0:T(8,128)S(1)} %bitcast.17), kind=kLoop, calls=%fused_computation.5 | loop fusion | flops 18874368 | bytes 30408704 | tf_op jit(solution)/shard_map/convert.1
  60.4 8.4 %pad_maximum_fusion = bf16[64,9,64,2,64]{4,2,3,1,0:T(8,128)(2,1)S(1)} fusion(bf16[64,9,64,1,64]{4,2,3,1,0:T(8,128)(2,1)} %get-tuple-element.43, bf16[64,9,64,1,64]{4,2,3,1,0:T(8,128)(2,1)S(1)} %get-tuple-element.42), kind=kLoop, calls=%fused_computation.3 | loop fusion | flops 4718592 | bytes 18874368 | tf_op jit(solution)/shard_map/while/body/eval_jaxpr/stack | solution.py:53
  68.8 17.8 %copy.22 = bf16[64,9,64,2,64]{4,3,2,1,0:T(2,128)(2,1)} copy(bf16[64,9,64,2,64]{4,2,3,1,0:T(8,128)(2,1)S(1)} %pad_maximum_fusion) | data formatting | bytes 18874368 | tf_op jit(solution)/shard_map/while/body/eval_jaxpr/stack | solution.py:53
  86.6 25.0 %convert_element_type.56 = bf16[576,8192]{1,0:T(8,128)(2,1)} reshape(bf16[64,9,64,2,64]{4,3,2,1,0:T(2,128)(2,1)} %copy.22) | data formatting | bytes 18874368 | tf_op jit(solution)/shard_map/while/body/eval_jaxpr/convert_element_type | solution.py:55
  111.5 15.8 %all-gather = bf16[4,4,8192]{2,1,0:T(4,128)(2,1)S(1)} all-gather(bf16[1,4,8192]{2,1,0:T(4,128)(2,1)S(1)} %bitcast.19), channel_id=1, replica_groups=mesh['half'=2,'panel'=4,'dom'=4] {'dom'}, dimensions={0}, use_global_device_ids=true | all-gather | bytes 327680 | tf_op jit(solution)/shard_map/all_gather | solution.py:125
  127.4 0.2 multiply_reduce_fusion
  127.9 6.3 %fusion.24 = (f32[576]{0:T(1024)S(1)}, f32[576,16]{0,1:T(8,128)S(1)}) fusion(f32[576]{0:T(1024)S(1)} %sub.101, f32[16]{0:T(128)S(1)} %broadcast_multiply_fusion.2, bf16[576,8192]{1,0:T(8,128)(2,1)} %convert_element_type.56, bf16[16,8192]{1,0:T(8,128)(2,1)S(1)} %reshape.246), kind=kOutput, calls=%fused_computation.53 | convolution fusion | flops 151022016 | bytes 9740864 | tf_op jit(solution)/shard_map/while/body/eval_jaxpr/dot_general | solution.py:70
  134.4 5.7 %pmax.7 = f32[64]{0:T(128)S(1)} all-reduce(f32[64]{0:T(128)S(1)} %reduce_max.18), channel_id=1, replica_groups=mesh['half'=2,'panel'=4,'dom'=4] {'panel'}, use_global_device_ids=true, to_apply=%region_3.4 | all-reduce | flops 64 | bytes 512 | tf_op jit(solution)/shard_map/pmax | solution.py:128
  140.2 0.1 sub.105
  140.6 6.6 %psum.7 = f32[64]{0:T(128)S(1)} all-reduce(f32[64]{0:T(128)S(1)} %reduce_sum.28), channel_id=1, replica_groups=mesh['half'=2,'panel'=4,'dom'=4] {'panel'}, use_global_device_ids=true, to_apply=%region_6.7 | all-reduce | flops 64 | bytes 512 | tf_op jit(solution)/shard_map/psum | solution.py:130
  147.3 0.1 div.35
  147.5 5.2 %fusion.6 = f32[16,8192]{1,0:T(8,128)S(1)} fusion(bf16[576,8192]{1,0:T(8,128)(2,1)} %convert_element_type.56, f32[576,16]{0,1:T(8,128)S(1)} %get-tuple-element.64, f32[576]{0:T(1024)S(1)} %div.35, f32[576]{0:T(1024)S(1)} %sub.105), kind=kOutput, calls=%fused_computation.18 | convolution fusion | flops 151022592 | bytes 10002944 | tf_op jit(solution)/shard_map/while/body/eval_jaxpr/while/body/eval_jaxpr/dot_general | solution.py:95
  153.0 2.2 scatter_custom_fusion
  155.2 0.5 log_add_fusion
  155.7 0.6 dynamic-slice.3
  157.0 86.3 %all-reduce.3.cloned.1.call-done = f32[32,1024]{1,0:T(8,128)} async-done(((f32[32,1024]{1,0:T(8,128)}), f32[32,1024]{1,0:T(8,128)}) %all-reduce.3.cloned.1.call-update) | async-done | bytes 131088
  243.3 1.4 dynamic-slice_multiply_fusion
  (31 shorter events, 1.6 us)
Async XLA Ops:
  7.2 236.1 %all-reduce.3.cloned.1.call-start = ((), (), s32[]{:S(2)}) async-start(), calls=%async_computation | async-start | bytes 262144
  22.6 7.7 %copy-start = (bf16[64,8192]{1,0:T(8,128)(2,1)S(1)}, bf16[64,8192]{1,0:T(8,128)(2,1)}, u32[]{:S(2)}) copy-start(bf16[64,8192]{1,0:T(8,128)(2,1)} %param.4) | copy-start | bytes 3145732
  86.6 25.0 %copy-start.1 = (bf16[4,8192]{1,0:T(4,128)(2,1)S(1)}, bf16[4,8192]{1,0:T(4,128)(2,1)}, u32[]{:S(2)}) copy-start(bf16[4,8192]{1,0:T(4,128)(2,1)} %param.6) | copy-start | bytes 196612
  134.2 18.6 %copy-start.2 = (s32[16,8]{0,1:T(8,128)S(1)}, s32[16,8]{0,1:T(8,128)}, u32[]{:S(2)}) copy-start(s32[16,8]{0,1:T(8,128)} %param.7) | copy-start | bytes 1540
  134.2 21.5 %copy-start.3 = (u32[32]{0:T(128)S(1)}, u32[32]{0:T(128)}, u32[]{:S(2)}) copy-start(u32[32]{0:T(128)} %constant.101) | copy-start | bytes 388
Sparse Core Ops, SparseCore 0:
  155.3 87.9 all-reduce.2
where the time goes:
time: 254 us; the launch traced here: 251 us
  waiting for transfers between devices  86.3 us (34%)
  local copies, waits for them, and re-layouts  72.7 us (29%)
  other arithmetic  37.9 us (15%)
  blocking collectives  28.2 us (11%)
  between operations  14.8 us (6%)
  matrix products  11.5 us (5%)
    unnamed x2, waiting for transfers between devices  86.3 us
    convert_element_type x1, local copies, waits for them, and re-layouts, shift_images(): return jnp.stack([out_real, out_imag], axis=3).reshape(row_count * SHIFTS...  25 us
    another operation x1, other arithmetic  17.8 us
    another operation x1, local copies, waits for them, and re-layouts, shift_images(): jnp.stack([out_real, out_imag], axis=3)  17.8 us
    all_gather x1, blocking collectives, shards(): gathered = lax.all_gather(references, 'dom', axis=0, tiled=True)  15.8 us
    another operation x1, other arithmetic, shift_images(): jnp.stack([out_real, out_imag], axis=3)  8.36 us
    gather x1, local copies, waits for them, and re-layouts, shift_images(): cosine = cos_table[shift_index]  7.91 us
    slice x1, local copies, waits for them, and re-layouts, shift_images(): real_part = picture[:, :, :, 0, :]  7.85 us
  transfers between devices with their start and end apart: 1, of which 1 were waited for; matrix products, arithmetic and copies ran while one was open for 0% of the time, Pallas kernels for 0%

commit v1 on v0

v1 whole, which is shorter than its diff:
```python
import functools
import math

import jax
import jax.numpy as jnp
from jax import lax
from jax.experimental import pallas as pl
from jax.experimental.pallas import tpu as pltpu
from jax.sharding import PartitionSpec as P

MESH = pl.DeviceIdType.MESH
PIX = 64
SHIFTS = 9
LANES = 128
TILE = 16
T_GROUP = 3
U_BLOCK = 8
PENALTY = 0.125
F32 = jnp.float32
BF16 = jnp.bfloat16
NT = (((1,), (1,)), ((), ()))


def row_offset(index):
    return (index * 37) >> 8


def kernel(
    n_panel, n_dom, scale, images, shift, refs, slots, vol_out, log_out,
    img, refs32, gathered, norms, moved, slot_all, part32, part16, landed, logs,
    img_sem, recv_sem, z_sem, y_sem, sib_sem, slot_send, slot_recv,
    part_send, part_recv, log_send, log_recv,
):
    n = n_panel * n_dom
    n_y = n_panel // 2
    panel, dom = lax.axis_index("panel"), lax.axis_index("dom")
    me = panel * n_dom + dom
    rows = img.shape[0]
    ref_rows = refs.shape[0]
    pieces = TILE // ref_rows
    width = gathered.shape[1]
    cols = gathered.shape[0]
    segments = slots.shape[1]
    seg_len = moved.shape[1] // segments
    block_total = 2 * n
    core = lax.rem(panel, 2)
    sibling = panel + 1 - 2 * core

    def y_peer(step):
        return lax.rem(panel + 2 * step, n_panel)

    def place(d):
        return {"panel": lax.div(d, n_dom), "dom": lax.rem(d, n_dom)}

    barrier = pltpu.get_barrier_semaphore()

    @pl.loop(1, n)
    def _(o):
        pl.semaphore_signal(barrier, inc=1, device_id=place(lax.rem(me + o, n)), device_id_type=MESH)

    first = pl.multiple_of(panel * rows, rows)
    img_copy = pltpu.make_async_copy(images.at[pl.ds(first, rows), :], img, img_sem)
    img_copy.start()

    def shard(d):
        return gathered.at[pl.ds(pl.multiple_of(d * TILE, TILE), TILE), :]

    for q in range(pieces):
        refs32[q * ref_rows:(q + 1) * ref_rows, :] = refs[:, q * width:(q + 1) * width].astype(F32)
    gathered[pl.ds(pl.multiple_of(me * TILE, TILE), TILE), :] = refs32[...].astype(BF16)
    slot_rows = slots.shape[0]
    slot_all[pl.ds(pl.multiple_of(panel * slot_rows, slot_rows), slot_rows), :] = jnp.zeros(
        (slot_rows, LANES), jnp.int32
    )
    slot_all[pl.ds(pl.multiple_of(panel * slot_rows, slot_rows), slot_rows), :segments] = slots[...]

    pl.semaphore_wait(barrier, n - 1)

    def shard_copy(d, device, sem):
        return pltpu.make_async_remote_copy(
            src_ref=shard(d), dst_ref=shard(d), send_sem=sem, recv_sem=recv_sem.at[d],
            device_id=device, device_id_type=MESH,
        )

    def right_copy(j):
        return shard_copy(panel * n_dom + j, {"dom": dom + 1}, z_sem.at[0, j])

    def left_copy(j):
        return shard_copy(panel * n_dom + j, {"dom": dom - 1}, z_sem.at[1, j])

    def y_copy(step, j):
        return shard_copy(panel * n_dom + j, {"panel": y_peer(step)}, y_sem.at[step - 1, j])

    def sib_copy(d):
        return shard_copy(d, {"panel": sibling}, sib_sem.at[d])

    def relay(j):
        for step in range(1, n_y):
            y_copy(step, j).start()
        sib_copy(panel * n_dom + j).start()

    def from_left(s):
        j = dom - s

        @pl.when(j >= 0)
        def _():
            if s > 0:
                sib_copy(panel * n_dom + j).wait_recv()

            @pl.when(dom + 1 < n_dom)
            def _():
                right_copy(j).start()

            if s > 0:
                relay(j)

    def from_right(s):
        j = dom + s

        @pl.when(j < n_dom)
        def _():
            if s > 0:
                sib_copy(panel * n_dom + j).wait_recv()

            @pl.when(dom >= 1)
            def _():
                left_copy(j).start()

            relay(j)

    def from_y(s):
        for step in range(1, n_y):
            base = y_peer(step) * n_dom

            def pass_on(j):
                sib_copy(base + j).wait_recv()
                sib_copy(base + j).start()

            if s > 0:
                pl.when(dom - s >= 0)(lambda: pass_on(dom - s))
            pl.when(dom + s < n_dom)(lambda: pass_on(dom + s))

    def slot_copy(step):
        own = slot_all.at[pl.ds(pl.multiple_of(panel * slot_rows, slot_rows), slot_rows), :]
        return pltpu.make_async_remote_copy(
            src_ref=own, dst_ref=own, send_sem=slot_send.at[step - 1], recv_sem=slot_recv.at[panel],
            device_id={"panel": lax.rem(panel + step, n_panel)}, device_id_type=MESH,
        )

    from_left(0)
    from_right(0)
    for step in range(1, n_panel):
        slot_copy(step).start()

    lane = lax.broadcasted_iota(jnp.int32, (rows, LANES), 1)
    turn_sign = jnp.where(lane < PIX, -1.0, 1.0).astype(F32)
    freq_col = (lane & (PIX - 1)) - PIX // 2

    def offsets(t):
        index = shift[pl.ds(first, rows), t:t + 1]
        a = row_offset(index)
        return a - 3, index - 7 * a - 3

    def shift_group(t0):
        angles, steps = [], []
        for t in range(t0, t0 + T_GROUP):
            a, b = offsets(t)
            turns = ((freq_col * b - (PIX // 2) * a + PIX // 2) & (PIX - 1)) - PIX // 2
            angles.append(turns.astype(F32) * (-2.0 * math.pi / PIX))
            steps.append(jnp.broadcast_to(a, (rows, LANES)).astype(F32) * (-2.0 * math.pi / PIX))
        angle = jnp.concatenate(angles, axis=0)
        turn = jnp.concatenate(steps, axis=0)
        sign = jnp.concatenate([turn_sign] * T_GROUP, axis=0)
        turn_cos, turn_sin = jnp.cos(turn), jnp.sin(turn) * sign

        def body(block, carry):
            cosine, sine = carry
            for k in range(U_BLOCK):
                at = pl.multiple_of((block * U_BLOCK + k) * LANES, LANES)
                x = img[:, pl.ds(at, LANES)].astype(F32)
                swapped = pltpu.roll(x, PIX, 1)
                x = jnp.concatenate([x] * T_GROUP, axis=0)
                swapped = jnp.concatenate([swapped] * T_GROUP, axis=0)
                moved[t0 * rows:(t0 + T_GROUP) * rows, pl.ds(at, LANES)] = (
                    x * cosine + swapped * sine
                ).astype(BF16)
                cosine, sine = cosine * turn_cos - sine * turn_sin, sine * turn_cos + cosine * turn_sin
            return cosine, sine

        lax.fori_loop(0, PIX // U_BLOCK, body, (jnp.cos(angle), jnp.sin(angle) * sign))

    img_copy.wait()
    groups = list(range(0, SHIFTS, T_GROUP))
    shift_group(groups[0])
    for s in range(1, n_dom):
        from_left(s)
        from_right(s)
        from_y(s - 1)
        if s < len(groups):
            shift_group(groups[s])
    for t0 in groups[max(n_dom, 1):]:
        shift_group(t0)
    from_y(n_dom - 1)
    for step in range(n_y):
        base = lax.rem(sibling + 2 * step, n_panel) * n_dom
        for j in range(n_dom):
            sib_copy(base + j).wait_recv()

    @pl.loop(0, n)
    def _(d):
        at = pl.ds(pl.multiple_of(d * TILE, TILE), TILE)
        total = jnp.zeros((TILE, LANES), F32)
        for k in range(width // LANES):
            value = gathered[at, k * LANES:(k + 1) * LANES].astype(F32)
            total += value * value
        norms[at, :] = total

    def fold(q, value):
        return value if q == 0 else pltpu.roll(value, cols - q * ref_rows, 1)

    scores = jnp.zeros((SHIFTS * rows, cols), F32)
    half_norm = -0.5 * jnp.sum(jnp.transpose(norms[...]), axis=0, keepdims=True)
    half_norm = jnp.broadcast_to(half_norm, (8, cols))
    norm_row = jnp.zeros((8, cols), F32)
    for q in range(pieces):
        product = lax.dot_general(
            moved[:, q * width:(q + 1) * width], gathered[...], NT, preferred_element_type=F32
        )
        scores += fold(q, product)
        norm_row += fold(q, half_norm)
    column = lax.broadcasted_iota(jnp.int32, (rows, cols), 1)
    valid = (column & (TILE - 1)) < ref_rows
    blocks = []
    for t in range(SHIFTS):
        a, b = offsets(t)
        cost = (a * a + b * b).astype(F32) * PENALTY
        block = scores[t * rows:(t + 1) * rows] + norm_row[:1] - cost
        blocks.append(jnp.where(valid, block, -jnp.inf))
    top = functools.reduce(jnp.maximum, blocks)
    top = jnp.max(top, axis=1, keepdims=True)
    blocks = [jnp.exp(block - top) for block in blocks]
    total = jnp.sum(sum(blocks), axis=1, keepdims=True)
    inverse = 1.0 / total
    weights = jnp.concatenate([(block * inverse).astype(BF16) for block in blocks], axis=0)

    evidence = top + jnp.log(total)
    spot = lax.broadcasted_iota(jnp.int32, (rows, LANES), 0) + panel * rows
    log_row = jnp.sum(jnp.where(lane == spot, evidence, 0.0), axis=0, keepdims=True)
    logs[panel] = jnp.broadcast_to(log_row, (8, LANES))

    def log_copy(step):
        return pltpu.make_async_remote_copy(
            src_ref=logs.at[panel], dst_ref=logs.at[panel], send_sem=log_send.at[step - 1],
            recv_sem=log_recv.at[panel],
            device_id={"panel": lax.rem(panel + step, n_panel)}, device_id_type=MESH,
        )

    for step in range(1, n_panel):
        log_copy(step).start()

    for step in range(1, n_panel):
        sender = lax.rem(panel + step, n_panel)
        landing = slot_all.at[pl.ds(pl.multiple_of(sender * slot_rows, slot_rows), slot_rows), :]
        pltpu.make_async_remote_copy(
            src_ref=landing, dst_ref=landing, send_sem=slot_send.at[step - 1], recv_sem=slot_recv.at[sender],
            device_id={"panel": sender}, device_id_type=MESH,
        ).wait_recv()
    ref_total = slot_all.shape[0]
    spread_col = lax.broadcasted_iota(jnp.int32, (ref_total, cols), 1)
    spread_row = lax.broadcasted_iota(jnp.int32, (ref_total, cols), 0)
    within = spread_col & (TILE - 1)
    spread_to = jnp.where(within < ref_rows, (spread_col >> 4) * ref_rows + within, -1)
    spread = jnp.where(spread_row == spread_to, 1.0, 0.0).astype(BF16)
    slot_t = jnp.transpose(slot_all[...].astype(F32))[:TILE].astype(BF16)
    slot_of = jnp.dot(slot_t, spread, preferred_element_type=F32)
    block_id = lax.broadcasted_iota(jnp.int32, (block_total, cols), 0).astype(F32)
    owner_rows = []
    for s in range(segments):
        owner_rows.append(jnp.where(block_id == slot_of[s:s + 1], 1.0, 0.0).astype(BF16))
    onehot = jnp.concatenate(owner_rows, axis=0)
    mixed = lax.dot_general(onehot, weights, NT, preferred_element_type=F32).astype(BF16)

    chunk = 2 * LANES
    lines = seg_len // LANES
    for c in range(seg_len // chunk):
        total = jnp.zeros((block_total, chunk), F32)
        for s in range(segments):
            at = s * seg_len + c * chunk
            total += jnp.dot(
                mixed[s * block_total:(s + 1) * block_total], moved[:, at:at + chunk],
                preferred_element_type=F32,
            )
        for k in range(2):
            part32[pl.ds(2 * c + k, block_total, stride=lines), :] = total[:, k * LANES:(k + 1) * LANES]
    part16[...] = part32[...].astype(BF16)

    def tile_of(ref, d):
        return ref.at[pl.ds(pl.multiple_of(d * TILE, TILE), TILE), :]

    def part_copy(d):
        return pltpu.make_async_remote_copy(
            src_ref=tile_of(part16, d), dst_ref=tile_of(landed, me), send_sem=part_send.at[d],
            recv_sem=part_recv.at[me], device_id=place(d), device_id_type=MESH,
        )

    def part_landing(d):
        return pltpu.make_async_remote_copy(
            src_ref=tile_of(part16, d), dst_ref=tile_of(landed, d), send_sem=part_send.at[d],
            recv_sem=part_recv.at[d], device_id=place(d), device_id_type=MESH,
        )

    @pl.loop(1, n)
    def _(o):
        part_copy(lax.rem(me + o, n)).start()

    def add_part(o, total):
        d = lax.rem(me + o, n)
        part_landing(d).wait_recv()
        return total + landed[pl.ds(pl.multiple_of(d * TILE, TILE), TILE), :].astype(F32)

    total = part32[pl.ds(pl.multiple_of(me * TILE, TILE), TILE), :]
    total = lax.fori_loop(1, n, add_part, total) * scale
    for k in range(TILE):
        vol_out[k // lines:k // lines + 1, (k % lines) * LANES:(k % lines + 1) * LANES] = total[k:k + 1]

    log_total = logs[panel]
    for step in range(1, n_panel):
        sender = lax.rem(panel + step, n_panel)
        pltpu.make_async_remote_copy(
            src_ref=logs.at[sender], dst_ref=logs.at[sender], send_sem=log_send.at[step - 1],
            recv_sem=log_recv.at[sender], device_id={"panel": sender}, device_id_type=MESH,
        ).wait_recv()
        log_total += logs[sender]
    log_out[...] = log_total[:1, :log_out.shape[1]]

    @pl.loop(1, n)
    def _(o):
        part_copy(lax.rem(me + o, n)).wait_send()

    for step in range(1, n_panel):
        slot_copy(step).wait_send()
        log_copy(step).wait_send()
    for j in range(n_dom):
        @pl.when((j <= dom) & (dom + 1 < n_dom))
        def _():
            right_copy(j).wait_send()

        @pl.when((j >= dom) & (dom >= 1))
        def _():
            left_copy(j).wait_send()

        for step in range(1, n_y):
            y_copy(step, j).wait_send()
        for step in range(n_y):
            sib_copy(y_peer(step) * n_dom + j).wait_send()


def shards(images, shift_index, references, slot_blocks):
    n_panel = lax.axis_size("panel")
    n_dom = lax.axis_size("dom")
    n = n_panel * n_dom
    part_dev, row_width = images.shape
    segments = slot_blocks.shape[1]
    block_total = 2 * n
    volume_scale = (part_dev * n_dom * segments / block_total) ** (-0.5)
    rows = part_dev // n_panel
    width = row_width * references.shape[0] // TILE
    seg_len = row_width // segments
    lines = seg_len // LANES
    vmem = pl.BlockSpec(memory_space=pltpu.VMEM)
    dma = pltpu.SemaphoreType.DMA
    volume, log_evidence = pl.pallas_call(
        functools.partial(kernel, n_panel, n_dom, volume_scale),
        out_shape=(
            jax.ShapeDtypeStruct((2, seg_len), F32),
            jax.ShapeDtypeStruct((1, part_dev), F32),
        ),
        in_specs=[pl.BlockSpec(memory_space=pl.ANY), vmem, vmem, vmem],
        out_specs=(vmem, vmem),
        scratch_shapes=[
            pltpu.VMEM((rows, row_width), BF16),
            pltpu.VMEM((TILE, width), F32),
            pltpu.VMEM((n * TILE, width), BF16),
            pltpu.VMEM((n * TILE, LANES), F32),
            pltpu.VMEM((SHIFTS * rows, row_width), BF16),
            pltpu.VMEM((n_panel * slot_blocks.shape[0], LANES), jnp.int32),
            pltpu.VMEM((block_total * lines, LANES), F32),
            pltpu.VMEM((block_total * lines, LANES), BF16),
            pltpu.VMEM((n * TILE, LANES), BF16),
            pltpu.VMEM((n_panel, 8, LANES), F32),
            dma(()),
            dma((n,)),
            dma((2, n_dom)),
            dma((max(n_panel // 2 - 1, 1), n_dom)),
            dma((n,)),
            dma((n_panel,)),
            dma((n_panel,)),
            dma((n,)),
            dma((n,)),
            dma((n_panel,)),
            dma((n_panel,)),
        ],
        compiler_params=pltpu.CompilerParams(
            collective_id=0, has_side_effects=True, vmem_limit_bytes=48 * 1024 * 1024
        ),
        name="expectation_backprojection",
    )(images, shift_index, references, slot_blocks)
    return volume, log_evidence.reshape(part_dev)


def solution(mesh):
    in_specs = (
        P(("half", "dom"), None),
        P(("half", "dom"), None),
        P(("half", "panel", "dom"), None),
        P(("half", "panel"), None),
    )
    out_specs = (P(("half", "panel", "dom"), None), P(("half", "dom")))
    return jax.shard_map(shards, mesh=mesh, in_specs=in_specs, out_specs=out_specs, check_vma=False)
```

time: 254 us -> 32.7 us (0.13)
  waiting for transfers between devices: 86.3 us -> 0 us
  local copies, waits for them, and re-layouts: 72.7 us -> 4.04 us
  other arithmetic: 37.9 us -> 0 us
  blocking collectives: 28.2 us -> 0 us
  Pallas kernels: 0 us -> 27.7 us
  between operations: 14.8 us -> 0.65 us
  matrix products: 11.5 us -> 0 us
    unnamed x2 -> x0, waiting for transfers between devices: 86.3 us -> none
    convert_element_type x2 -> x0, local copies, waits for them, and re-layouts: 29.4 us -> none  [the longest x1 25 us: shift_images(): return jnp.stack([out_real, out_imag], axis=3).reshape(row_count * SHIFTS...]
    pallas_call x0 -> x1, Pallas kernels: none -> 27.7 us  [shards(): pl.pallas_call(functools.partial(kernel, n_panel, n_dom, volume_scale), o...]
    another operation x2 -> x0, other arithmetic: 26.2 us -> none
    another operation x1 -> x0, local copies, waits for them, and re-layouts: 17.8 us -> none  [shift_images(): jnp.stack([out_real, out_imag], axis=3)]
    all_gather x1 -> x0, blocking collectives: 15.8 us -> none  [shards(): gathered = lax.all_gather(references, 'dom', axis=0, tiled=True)]
    gather x2 -> x0, local copies, waits for them, and re-layouts: 15.6 us -> none  [the longest x1 7.91 us: shift_images(): cosine = cos_table[shift_index]]
    dot_general x2 -> x0, matrix products: 11.5 us -> none  [the longest x1 6.31 us: one_block(): lax.dot_general(moved, gathered, (((1,), (1,)), ((), ())), preferred_elem...]
  transfers between devices with their start and end apart: 1 -> 0, of which waited for: 1 -> 0; matrix products, arithmetic and copies ran while one was open for 0% -> 0% of each run, Pallas kernels for 0% -> 0%
where the time goes in v1:
time: 32.7 us; the launch traced here: 32.4 us
  Pallas kernels  27.7 us (85%)
  local copies, waits for them, and re-layouts  4.04 us (12%)
  between operations  0.65 us (2%)
    pallas_call x1, Pallas kernels, shards(): pl.pallas_call(functools.partial(kernel, n_panel, n_dom, volume_scale), o...  27.7 us
    unnamed x10, local copies, waits for them, and re-layouts  4.04 us

profile of v1, /device:TPU:0, one launch (start us, length us, event | category | flops | bytes accessed | tf_op | source)
XLA Modules:
  0.0 32.4 jit_solution(14874960578255167316)
XLA Ops:
  0.6 0.0 copy-start.2
  0.6 0.8 %copy.7.slots = s32[16,8]{1,0:T(8,128)S(1)} copy(s32[16,8]{0,1:T(8,128)} %param.7) | data formatting | bytes 1024 | tf_op args[3]
  1.4 0.0 copy-done.2
  1.4 0.1 copy.6.shift
  1.5 0.0 copy-start
  1.5 1.2 %copy-done = bf16[64,8192]{1,0:T(8,128)(2,1)S(1)} copy-done((bf16[64,8192]{1,0:T(8,128)(2,1)S(1)}, bf16[64,8192]{1,0:T(8,128)(2,1)}, u32[]{:S(2)}) %copy-start) | copy-done | bytes 1048600
  2.7 0.0 copy-start.1
  2.7 0.8 %copy-done.1 = bf16[4,8192]{1,0:T(4,128)(2,1)S(1)} copy-done((bf16[4,8192]{1,0:T(4,128)(2,1)S(1)}, bf16[4,8192]{1,0:T(4,128)(2,1)}, u32[]{:S(2)}) %copy-start.1) | copy-done | bytes 65560
  3.6 27.7 %expectation_backprojection.1 = (f32[2,1024]{1,0:T(2,128)S(1)}, f32[1,64]{1,0:T(1,128)S(1)}) custom-call(bf16[64,8192]{1,0:T(8,128)(2,1)S(1)} %copy-done, s32[64,9]{1,0:T(8,128)S(1)} %copy.6.shift, bf16[4,8192]{1,0:T(4,128)(2,1)S(1)} %copy-done.1, s32[16,8]{1,0:T(8,128)S(1)} %copy.7.slots), custom_call_target="tpu_custom_call" | custom-call | tf_op jit(solution)/shard_map/expectation_backprojection/pallas_call | solution.py:372
  31.3 0.6 %copy.10 = f32[2,1024]{1,0:T(2,128)} copy(f32[2,1024]{1,0:T(2,128)S(1)} %get-tuple-element.8) | data formatting | bytes 16384
  31.9 0.5 %copy.11 = f32[64]{0:T(128)} copy(f32[64]{0:T(128)S(1)} %bitcast.1) | data formatting | bytes 512
Async XLA Ops:
  0.6 0.8 %copy-start.2 = (s32[64,9]{0,1:T(8,128)S(1)}, s32[64,9]{0,1:T(8,128)}, u32[]{:S(2)}) copy-start(s32[64,9]{0,1:T(8,128)} %param.5) | copy-start | bytes 6916
  1.5 1.2 %copy-start = (bf16[64,8192]{1,0:T(8,128)(2,1)S(1)}, bf16[64,8192]{1,0:T(8,128)(2,1)}, u32[]{:S(2)}) copy-start(bf16[64,8192]{1,0:T(8,128)(2,1)} %images.1) | copy-start | bytes 3145732
  2.7 0.8 %copy-start.1 = (bf16[4,8192]{1,0:T(4,128)(2,1)S(1)}, bf16[4,8192]{1,0:T(4,128)(2,1)}, u32[]{:S(2)}) copy-start(bf16[4,8192]{1,0:T(4,128)(2,1)} %refs.1) | copy-start | bytes 196612

commit v2 on v1

--- a/solution.py
+++ b/solution.py
@@ -27,8 +27,8 @@
 
 def kernel(
     n_panel, n_dom, scale, images, shift, refs, slots, vol_out, log_out,
-    img, refs32, gathered, norms, moved, slot_all, part32, part16, landed, logs,
-    img_sem, recv_sem, z_sem, y_sem, sib_sem, slot_send, slot_recv,
+    img, refs_in, shift_in, shift_pad, shift_col, refs32, gathered, norms, moved, slot_in, slot_all, onehot,
+    part32, part16, landed, logs, in_sem, recv_sem, z_sem, y_sem, sib_sem, slot_send, slot_recv,
     part_send, part_recv, log_send, log_recv,
 ):
     n = n_panel * n_dom
@@ -40,8 +40,9 @@
     pieces = TILE // ref_rows
     width = gathered.shape[1]
     cols = gathered.shape[0]
-    segments = slots.shape[1]
-    seg_len = moved.shape[1] // segments
+    cands = SHIFTS * rows
+    segments = slots.shape[0]
+    seg_len = img.shape[1] // segments
     block_total = 2 * n
     core = lax.rem(panel, 2)
     sibling = panel + 1 - 2 * core
@@ -52,27 +53,40 @@
     def place(d):
         return {"panel": lax.div(d, n_dom), "dom": lax.rem(d, n_dom)}
 
+    first = pl.multiple_of(panel * rows, rows)
+    refs_copy = pltpu.make_async_copy(refs, refs_in, in_sem.at[0])
+    img_copy = pltpu.make_async_copy(images.at[pl.ds(first, rows), :], img, in_sem.at[1])
+    shift_copy = pltpu.make_async_copy(shift, shift_in, in_sem.at[2])
+    slot_load = pltpu.make_async_copy(slots, slot_in, in_sem.at[3])
+    refs_copy.start()
+    shift_copy.start()
+    slot_load.start()
+    img_copy.start()
+
     barrier = pltpu.get_barrier_semaphore()
 
     @pl.loop(1, n)
     def _(o):
         pl.semaphore_signal(barrier, inc=1, device_id=place(lax.rem(me + o, n)), device_id_type=MESH)
 
-    first = pl.multiple_of(panel * rows, rows)
-    img_copy = pltpu.make_async_copy(images.at[pl.ds(first, rows), :], img, img_sem)
-    img_copy.start()
-
     def shard(d):
         return gathered.at[pl.ds(pl.multiple_of(d * TILE, TILE), TILE), :]
 
+    def add_norm(d):
+        at = pl.ds(pl.multiple_of(d * TILE, TILE), TILE)
+        total = jnp.zeros((TILE, LANES), F32)
+        for k in range(width // LANES):
+            value = gathered[at, k * LANES:(k + 1) * LANES].astype(F32)
+            total += value * value
+        norms[at, :] = total
+
+    refs_copy.wait()
     for q in range(pieces):
-        refs32[q * ref_rows:(q + 1) * ref_rows, :] = refs[:, q * width:(q + 1) * width].astype(F32)
+        refs32[q * ref_rows:(q + 1) * ref_rows, :] = refs_in[:, q * width:(q + 1) * width].astype(F32)
     gathered[pl.ds(pl.multiple_of(me * TILE, TILE), TILE), :] = refs32[...].astype(BF16)
-    slot_rows = slots.shape[0]
-    slot_all[pl.ds(pl.multiple_of(panel * slot_rows, slot_rows), slot_rows), :] = jnp.zeros(
-        (slot_rows, LANES), jnp.int32
-    )
-    slot_all[pl.ds(pl.multiple_of(panel * slot_rows, slot_rows), slot_rows), :segments] = slots[...]
+    slot_load.wait()
+    slot_all[panel] = jnp.zeros((segments, LANES), jnp.int32)
+    slot_all[panel, :, :slots.shape[1]] = slot_in[...]
 
     pl.semaphore_wait(barrier, n - 1)
 
@@ -113,6 +127,7 @@
 
             if s > 0:
                 relay(j)
+                add_norm(panel * n_dom + j)
 
     def from_right(s):
         j = dom + s
@@ -127,6 +142,7 @@
                 left_copy(j).start()
 
             relay(j)
+            add_norm(panel * n_dom + j)
 
     def from_y(s):
         for step in range(1, n_y):
@@ -135,13 +151,14 @@
             def pass_on(j):
                 sib_copy(base + j).wait_recv()
                 sib_copy(base + j).start()
+                add_norm(base + j)
 
             if s > 0:
                 pl.when(dom - s >= 0)(lambda: pass_on(dom - s))
             pl.when(dom + s < n_dom)(lambda: pass_on(dom + s))
 
     def slot_copy(step):
-        own = slot_all.at[pl.ds(pl.multiple_of(panel * slot_rows, slot_rows), slot_rows), :]
+        own = slot_all.at[panel]
         return pltpu.make_async_remote_copy(
             src_ref=own, dst_ref=own, send_sem=slot_send.at[step - 1], recv_sem=slot_recv.at[panel],
             device_id={"panel": lax.rem(panel + step, n_panel)}, device_id_type=MESH,
@@ -156,38 +173,85 @@
     turn_sign = jnp.where(lane < PIX, -1.0, 1.0).astype(F32)
     freq_col = (lane & (PIX - 1)) - PIX // 2
 
+    shift_copy.wait()
+    shift_pad[...] = jnp.zeros(shift_pad.shape, F32)
+    shift_pad[:SHIFTS, :shift.shape[1]] = shift_in[...].astype(F32)
+    shift_col[...] = jnp.transpose(shift_pad[...]).astype(jnp.int32)
+
+    multiple = lax.broadcasted_iota(jnp.int32, (8, LANES), 0)
+    turns = (freq_col[:8] * multiple + PIX // 2) & (PIX - 1)
+    angle = (turns - PIX // 2).astype(F32) * (-2.0 * math.pi / PIX)
+    cos_rows, sin_rows = jnp.cos(angle), jnp.sin(angle)
+
     def offsets(t):
-        index = shift[pl.ds(first, rows), t:t + 1]
+        index = shift_col[pl.ds(first, rows), t:t + 1]
         a = row_offset(index)
         return a - 3, index - 7 * a - 3
 
+    def pick(k, options):
+        out = options[0]
+        for i in range(1, len(options)):
+            out = jnp.where(k == i, options[i], out)
+        return out
+
+    blocks_per_piece = width // (U_BLOCK * LANES)
+
     def shift_group(t0):
-        angles, steps = [], []
+        parts = []
         for t in range(t0, t0 + T_GROUP):
             a, b = offsets(t)
-            turns = ((freq_col * b - (PIX // 2) * a + PIX // 2) & (PIX - 1)) - PIX // 2
-            angles.append(turns.astype(F32) * (-2.0 * math.pi / PIX))
-            steps.append(jnp.broadcast_to(a, (rows, LANES)).astype(F32) * (-2.0 * math.pi / PIX))
-        angle = jnp.concatenate(angles, axis=0)
-        turn = jnp.concatenate(steps, axis=0)
-        sign = jnp.concatenate([turn_sign] * T_GROUP, axis=0)
-        turn_cos, turn_sin = jnp.cos(turn), jnp.sin(turn) * sign
+            a = jnp.broadcast_to(a, (rows, LANES))
+            b = jnp.broadcast_to(b, (rows, LANES))
+            flip = jnp.where((a & 1) == 1, -1.0, 1.0).astype(F32)
+            far_a, far_b = jnp.abs(a), jnp.abs(b)
+            cosine = flip * pick(far_b, [cos_rows[k:k + 1] for k in range(4)])
+            sine = flip * pick(far_b, [sin_rows[k:k + 1] for k in range(4)]) * turn_sign
+            sine = jnp.where(b < 0, -sine, sine)
+            turn_cos = pick(far_a, [jnp.full((rows, LANES), math.cos(2 * math.pi * k / PIX), F32) for k in range(4)])
+            turn_sin = pick(far_a, [jnp.full((rows, LANES), math.sin(2 * math.pi * k / PIX), F32) for k in range(4)])
+            turn_sin = jnp.where(a < 0, turn_sin, -turn_sin) * turn_sign
+            parts.append((cosine, sine, turn_cos, turn_sin))
+        cosine, sine, turn_cos, turn_sin = (jnp.concatenate(x, axis=0) for x in zip(*parts))
 
         def body(block, carry):
             cosine, sine = carry
+            q = lax.div(block, blocks_per_piece)
+            lane0 = lax.rem(block, blocks_per_piece) * (U_BLOCK * LANES)
+            at_rows = pl.ds(pl.multiple_of(q * cands + t0 * rows, rows), T_GROUP * rows)
             for k in range(U_BLOCK):
                 at = pl.multiple_of((block * U_BLOCK + k) * LANES, LANES)
+                to = pl.multiple_of(lane0 + k * LANES, LANES)
                 x = img[:, pl.ds(at, LANES)].astype(F32)
                 swapped = pltpu.roll(x, PIX, 1)
                 x = jnp.concatenate([x] * T_GROUP, axis=0)
                 swapped = jnp.concatenate([swapped] * T_GROUP, axis=0)
-                moved[t0 * rows:(t0 + T_GROUP) * rows, pl.ds(at, LANES)] = (
-                    x * cosine + swapped * sine
-                ).astype(BF16)
+                moved[at_rows, pl.ds(to, LANES)] = (x * cosine + swapped * sine).astype(BF16)
                 cosine, sine = cosine * turn_cos - sine * turn_sin, sine * turn_cos + cosine * turn_sin
             return cosine, sine
 
-        lax.fori_loop(0, PIX // U_BLOCK, body, (jnp.cos(angle), jnp.sin(angle) * sign))
+        lax.fori_loop(0, PIX // U_BLOCK, body, (cosine, sine))
+
+    def build_onehot():
+        for step in range(1, n_panel):
+            sender = lax.rem(panel + step, n_panel)
+            pltpu.make_async_remote_copy(
+                src_ref=slot_all.at[sender], dst_ref=slot_all.at[sender], send_sem=slot_send.at[step - 1],
+                recv_sem=slot_recv.at[sender], device_id={"panel": sender}, device_id_type=MESH,
+            ).wait_recv()
+        spread_col = lax.broadcasted_iota(jnp.int32, (LANES, cols), 1)
+        spread_row = lax.broadcasted_iota(jnp.int32, (LANES, cols), 0)
+        within = spread_col & (TILE - 1)
+        spread_to = jnp.where(within < ref_rows, (spread_col >> 4) * ref_rows + within, -1)
+        slot_of = jnp.zeros((segments, cols), F32)
+        for k in range(n_panel):
+            spread = jnp.where(spread_row + k * slots.shape[1] == spread_to, 1.0, 0.0)
+            spread = jnp.where(spread_row < slots.shape[1], spread, 0.0).astype(BF16)
+            slot_of += jnp.dot(slot_all[k].astype(F32).astype(BF16), spread, preferred_element_type=F32)
+        block_id = lax.broadcasted_iota(jnp.int32, (block_total, cols), 0).astype(F32)
+        for s in range(segments):
+            onehot[s * block_total:(s + 1) * block_total, :] = jnp.where(
+                block_id == slot_of[s:s + 1], 1.0, 0.0
+            ).astype(BF16)
 
     img_copy.wait()
     groups = list(range(0, SHIFTS, T_GROUP))
@@ -198,22 +262,19 @@
         from_y(s - 1)
         if s < len(groups):
             shift_group(groups[s])
+        else:
+            if s == len(groups):
+                build_onehot()
     for t0 in groups[max(n_dom, 1):]:
         shift_group(t0)
+    if n_dom <= len(groups):
+        build_onehot()
     from_y(n_dom - 1)
     for step in range(n_y):
         base = lax.rem(sibling + 2 * step, n_panel) * n_dom
         for j in range(n_dom):
             sib_copy(base + j).wait_recv()
-
-    @pl.loop(0, n)
-    def _(d):
-        at = pl.ds(pl.multiple_of(d * TILE, TILE), TILE)
-        total = jnp.zeros((TILE, LANES), F32)
-        for k in range(width // LANES):
-            value = gathered[at, k * LANES:(k + 1) * LANES].astype(F32)
-            total += value * value
-        norms[at, :] = total
+            add_norm(base + j)
 
     def fold(q, value):
         return value if q == 0 else pltpu.roll(value, cols - q * ref_rows, 1)
@@ -222,11 +283,9 @@
     half_norm = -0.5 * jnp.sum(jnp.transpose(norms[...]), axis=0, keepdims=True)
     half_norm = jnp.broadcast_to(half_norm, (8, cols))
     norm_row = jnp.zeros((8, cols), F32)
+    product = lax.dot_general(moved[...], gathered[...], NT, preferred_element_type=F32)
     for q in range(pieces):
-        product = lax.dot_general(
-            moved[:, q * width:(q + 1) * width], gathered[...], NT, preferred_element_type=F32
-        )
-        scores += fold(q, product)
+        scores += fold(q, product[q * cands:(q + 1) * cands])
         norm_row += fold(q, half_norm)
     column = lax.broadcasted_iota(jnp.int32, (rows, cols), 1)
     valid = (column & (TILE - 1)) < ref_rows
@@ -258,36 +317,16 @@
     for step in range(1, n_panel):
         log_copy(step).start()
 
-    for step in range(1, n_panel):
-        sender = lax.rem(panel + step, n_panel)
-        landing = slot_all.at[pl.ds(pl.multiple_of(sender * slot_rows, slot_rows), slot_rows), :]
-        pltpu.make_async_remote_copy(
-            src_ref=landing, dst_ref=landing, send_sem=slot_send.at[step - 1], recv_sem=slot_recv.at[sender],
-            device_id={"panel": sender}, device_id_type=MESH,
-        ).wait_recv()
-    ref_total = slot_all.shape[0]
-    spread_col = lax.broadcasted_iota(jnp.int32, (ref_total, cols), 1)
-    spread_row = lax.broadcasted_iota(jnp.int32, (ref_total, cols), 0)
-    within = spread_col & (TILE - 1)
-    spread_to = jnp.where(within < ref_rows, (spread_col >> 4) * ref_rows + within, -1)
-    spread = jnp.where(spread_row == spread_to, 1.0, 0.0).astype(BF16)
-    slot_t = jnp.transpose(slot_all[...].astype(F32))[:TILE].astype(BF16)
-    slot_of = jnp.dot(slot_t, spread, preferred_element_type=F32)
-    block_id = lax.broadcasted_iota(jnp.int32, (block_total, cols), 0).astype(F32)
-    owner_rows = []
-    for s in range(segments):
-        owner_rows.append(jnp.where(block_id == slot_of[s:s + 1], 1.0, 0.0).astype(BF16))
-    onehot = jnp.concatenate(owner_rows, axis=0)
-    mixed = lax.dot_general(onehot, weights, NT, preferred_element_type=F32).astype(BF16)
+    mixed = lax.dot_general(onehot[...], weights, NT, preferred_element_type=F32).astype(BF16)
 
     chunk = 2 * LANES
     lines = seg_len // LANES
     for c in range(seg_len // chunk):
         total = jnp.zeros((block_total, chunk), F32)
         for s in range(segments):
-            at = s * seg_len + c * chunk
+            q, at = divmod(s * seg_len + c * chunk, width)
             total += jnp.dot(
-                mixed[s * block_total:(s + 1) * block_total], moved[:, at:at + chunk],
+                mixed[s * block_total:(s + 1) * block_total], moved[q * cands:(q + 1) * cands, at:at + chunk],
                 preferred_element_type=F32,
             )
         for k in range(2):
@@ -360,7 +399,7 @@
     n_dom = lax.axis_size("dom")
     n = n_panel * n_dom
     part_dev, row_width = images.shape
-    segments = slot_blocks.shape[1]
+    slot_rows, segments = slot_blocks.shape
     block_total = 2 * n
     volume_scale = (part_dev * n_dom * segments / block_total) ** (-0.5)
     rows = part_dev // n_panel
@@ -375,20 +414,26 @@
             jax.ShapeDtypeStruct((2, seg_len), F32),
             jax.ShapeDtypeStruct((1, part_dev), F32),
         ),
-        in_specs=[pl.BlockSpec(memory_space=pl.ANY), vmem, vmem, vmem],
+        in_specs=[pl.BlockSpec(memory_space=pltpu.HBM)] * 4,
         out_specs=(vmem, vmem),
         scratch_shapes=[
             pltpu.VMEM((rows, row_width), BF16),
+            pltpu.VMEM(references.shape, BF16),
+            pltpu.VMEM((SHIFTS, part_dev), jnp.int32),
+            pltpu.VMEM((TILE, LANES), F32),
+            pltpu.VMEM((LANES, TILE), jnp.int32),
             pltpu.VMEM((TILE, width), F32),
             pltpu.VMEM((n * TILE, width), BF16),
             pltpu.VMEM((n * TILE, LANES), F32),
-            pltpu.VMEM((SHIFTS * rows, row_width), BF16),
-            pltpu.VMEM((n_panel * slot_blocks.shape[0], LANES), jnp.int32),
+            pltpu.VMEM((SHIFTS * rows * (row_width // width), width), BF16),
+            pltpu.VMEM((segments, slot_rows), jnp.int32),
+            pltpu.VMEM((n_panel, segments, LANES), jnp.int32),
+            pltpu.VMEM((segments * block_total, n * TILE), BF16),
             pltpu.VMEM((block_total * lines, LANES), F32),
             pltpu.VMEM((block_total * lines, LANES), BF16),
             pltpu.VMEM((n * TILE, LANES), BF16),
             pltpu.VMEM((n_panel, 8, LANES), F32),
-            dma(()),
+            dma((4,)),
             dma((n,)),
             dma((2, n_dom)),
             dma((max(n_panel // 2 - 1, 1), n_dom)),
@@ -401,10 +446,10 @@
             dma((n_panel,)),
         ],
         compiler_params=pltpu.CompilerParams(
-            collective_id=0, has_side_effects=True, vmem_limit_bytes=48 * 1024 * 1024
+            collective_id=0, has_side_effects=True, vmem_limit_bytes=56 * 1024 * 1024
         ),
         name="expectation_backprojection",
-    )(images, shift_index, references, slot_blocks)
+    )(images, shift_index.T, references, slot_blocks.T)
     return volume, log_evidence.reshape(part_dev)
 
 

time: 32.7 us -> 30.6 us (0.936)
  local copies, waits for them, and re-layouts: 4.04 us -> 1.81 us
    unnamed x10 -> x4, local copies, waits for them, and re-layouts: 4.04 us -> 1.81 us
where the time goes in v2:
time: 30.6 us; the launch traced here: 30.4 us
  Pallas kernels  27.9 us (91%)
  local copies, waits for them, and re-layouts  1.81 us (6%)
  between operations  0.65 us (2%)
    pallas_call x1, Pallas kernels, shards(): pl.pallas_call(functools.partial(kernel, n_panel, n_dom, volume_scale), o...  27.9 us
    unnamed x4, local copies, waits for them, and re-layouts  1.81 us

profile of v2, /device:TPU:0, one launch (start us, length us, event | category | flops | bytes accessed | tf_op | source)
XLA Modules:
  0.0 30.4 jit_solution(17308984354955214017)
XLA Ops:
  0.6 27.9 %expectation_backprojection.1 = (f32[2,1024]{1,0:T(2,128)}, f32[1,64]{1,0:T(1,128)}) custom-call(bf16[64,8192]{1,0:T(8,128)(2,1)} %images.1, s32[9,64]{1,0:T(8,128)} %bitcast.3, bf16[4,8192]{1,0:T(4,128)(2,1)} %refs.1, s32[8,16]{1,0:T(8,128)} %bitcast.4), custom_call_target="tpu_custom_call" | custom-call | tf_op jit(solution)/shard_map/expectation_backprojection/pallas_call | solution.py:411
  28.6 0.0 copy-start
  28.6 1.3 %copy.8 = f32[2,1024]{1,0:T(2,128)} copy(f32[2,1024]{1,0:T(2,128)} %get-tuple-element.8) | data formatting | bytes 16384
  29.9 0.0 copy-done
  29.9 0.5 %copy.9 = f32[64]{0:T(128)} copy(f32[64]{0:T(128)S(1)} %bitcast.5) | data formatting | bytes 512
Async XLA Ops:
  28.6 1.3 %copy-start = (f32[1,64]{1,0:T(1,128)S(1)}, f32[1,64]{1,0:T(1,128)}, u32[]{:S(2)}) copy-start(f32[1,64]{1,0:T(1,128)} %get-tuple-element.5) | copy-start | bytes 772

commit v3 on v2

--- a/solution.py
+++ b/solution.py
@@ -65,9 +65,16 @@
 
     barrier = pltpu.get_barrier_semaphore()
 
-    @pl.loop(1, n)
+    @pl.loop(1, n_dom)
     def _(o):
-        pl.semaphore_signal(barrier, inc=1, device_id=place(lax.rem(me + o, n)), device_id_type=MESH)
+        pl.semaphore_signal(
+            barrier, inc=1, device_id={"dom": lax.rem(dom + o, n_dom)}, device_id_type=MESH
+        )
+
+    for step in range(1, n_panel):
+        pl.semaphore_signal(
+            barrier, inc=1, device_id={"panel": lax.rem(panel + step, n_panel)}, device_id_type=MESH
+        )
 
     def shard(d):
         return gathered.at[pl.ds(pl.multiple_of(d * TILE, TILE), TILE), :]
@@ -88,7 +95,7 @@
     slot_all[panel] = jnp.zeros((segments, LANES), jnp.int32)
     slot_all[panel, :, :slots.shape[1]] = slot_in[...]
 
-    pl.semaphore_wait(barrier, n - 1)
+    pl.semaphore_wait(barrier, n_dom + n_panel - 2)
 
     def shard_copy(d, device, sem):
         return pltpu.make_async_remote_copy(
@@ -96,11 +103,8 @@
             device_id=device, device_id_type=MESH,
         )
 
-    def right_copy(j):
-        return shard_copy(panel * n_dom + j, {"dom": dom + 1}, z_sem.at[0, j])
-
-    def left_copy(j):
-        return shard_copy(panel * n_dom + j, {"dom": dom - 1}, z_sem.at[1, j])
+    def line_copy(target):
+        return shard_copy(me, {"dom": target}, z_sem.at[target])
 
     def y_copy(step, j):
         return shard_copy(panel * n_dom + j, {"panel": y_peer(step)}, y_sem.at[step - 1, j])
@@ -113,36 +117,14 @@
             y_copy(step, j).start()
         sib_copy(panel * n_dom + j).start()
 
-    def from_left(s):
-        j = dom - s
-
-        @pl.when(j >= 0)
-        def _():
-            if s > 0:
-                sib_copy(panel * n_dom + j).wait_recv()
-
-            @pl.when(dom + 1 < n_dom)
-            def _():
-                right_copy(j).start()
-
-            if s > 0:
-                relay(j)
-                add_norm(panel * n_dom + j)
-
-    def from_right(s):
-        j = dom + s
-
-        @pl.when(j < n_dom)
-        def _():
-            if s > 0:
-                sib_copy(panel * n_dom + j).wait_recv()
-
-            @pl.when(dom >= 1)
-            def _():
-                left_copy(j).start()
-
-            relay(j)
-            add_norm(panel * n_dom + j)
+    def from_line(j):
+        sib_copy(panel * n_dom + j).wait_recv()
+        relay(j)
+        add_norm(panel * n_dom + j)
+
+    def at_distance(s, do):
+        pl.when(dom - s >= 0)(lambda: do(dom - s))
+        pl.when(dom + s < n_dom)(lambda: do(dom + s))
 
     def from_y(s):
         for step in range(1, n_y):
@@ -154,8 +136,9 @@
                 add_norm(base + j)
 
             if s > 0:
-                pl.when(dom - s >= 0)(lambda: pass_on(dom - s))
-            pl.when(dom + s < n_dom)(lambda: pass_on(dom + s))
+                at_distance(s, pass_on)
+            else:
+                pass_on(dom)
 
     def slot_copy(step):
         own = slot_all.at[panel]
@@ -164,8 +147,9 @@
             device_id={"panel": lax.rem(panel + step, n_panel)}, device_id_type=MESH,
         )
 
-    from_left(0)
-    from_right(0)
+    relay(dom)
+    for s in range(1, n_dom):
+        at_distance(s, lambda target: line_copy(target).start())
     for step in range(1, n_panel):
         slot_copy(step).start()
 
@@ -254,20 +238,15 @@
             ).astype(BF16)
 
     img_copy.wait()
-    groups = list(range(0, SHIFTS, T_GROUP))
-    shift_group(groups[0])
+    for t0 in range(0, SHIFTS, T_GROUP):
+        shift_group(t0)
+    add_norm(me)
     for s in range(1, n_dom):
-        from_left(s)
-        from_right(s)
+        at_distance(s, from_line)
         from_y(s - 1)
-        if s < len(groups):
-            shift_group(groups[s])
-        else:
-            if s == len(groups):
-                build_onehot()
-    for t0 in groups[max(n_dom, 1):]:
-        shift_group(t0)
-    if n_dom <= len(groups):
+        if s == 1:
+            build_onehot()
+    if n_dom == 1:
         build_onehot()
     from_y(n_dom - 1)
     for step in range(n_y):
@@ -380,13 +359,9 @@
         slot_copy(step).wait_send()
         log_copy(step).wait_send()
     for j in range(n_dom):
-        @pl.when((j <= dom) & (dom + 1 < n_dom))
+        @pl.when(j != dom)
         def _():
-            right_copy(j).wait_send()
-
-        @pl.when((j >= dom) & (dom >= 1))
-        def _():
-            left_copy(j).wait_send()
+            line_copy(j).wait_send()
 
         for step in range(1, n_y):
             y_copy(step, j).wait_send()
@@ -435,7 +410,7 @@
             pltpu.VMEM((n_panel, 8, LANES), F32),
             dma((4,)),
             dma((n,)),
-            dma((2, n_dom)),
+            dma((n_dom,)),
             dma((max(n_panel // 2 - 1, 1), n_dom)),
             dma((n,)),
             dma((n_panel,)),

time: 30.6 us -> 27.7 us (0.905)
  Pallas kernels: 27.9 us -> 25.1 us
    pallas_call x1, Pallas kernels: 27.9 us -> 25.1 us  [shards(): pl.pallas_call(functools.partial(kernel, n_panel, n_dom, volume_scale), o...]
where the time goes in v3:
time: 27.7 us; the launch traced here: 27.6 us
  Pallas kernels  25.1 us (91%)
  local copies, waits for them, and re-layouts  1.81 us (7%)
  between operations  0.65 us (2%)
    pallas_call x1, Pallas kernels, shards(): pl.pallas_call(functools.partial(kernel, n_panel, n_dom, volume_scale), o...  25.1 us
    unnamed x4, local copies, waits for them, and re-layouts  1.81 us

profile of v3, /device:TPU:0, one launch (start us, length us, event | category | flops | bytes accessed | tf_op | source)
XLA Modules:
  0.0 27.6 jit_solution(12346185141598553427)
XLA Ops:
  0.6 25.1 %expectation_backprojection.1 = (f32[2,1024]{1,0:T(2,128)}, f32[1,64]{1,0:T(1,128)}) custom-call(bf16[64,8192]{1,0:T(8,128)(2,1)} %images.1, s32[9,64]{1,0:T(8,128)} %bitcast.3, bf16[4,8192]{1,0:T(4,128)(2,1)} %refs.1, s32[8,16]{1,0:T(8,128)} %bitcast.4), custom_call_target="tpu_custom_call" | custom-call | tf_op jit(solution)/shard_map/expectation_backprojection/pallas_call | solution.py:386
  25.7 0.0 copy-start
  25.7 1.3 %copy.8 = f32[2,1024]{1,0:T(2,128)} copy(f32[2,1024]{1,0:T(2,128)} %get-tuple-element.8) | data formatting | bytes 16384
  27.0 0.0 copy-done
  27.0 0.5 %copy.9 = f32[64]{0:T(128)} copy(f32[64]{0:T(128)S(1)} %bitcast.5) | data formatting | bytes 512
Async XLA Ops:
  25.7 1.3 %copy-start = (f32[1,64]{1,0:T(1,128)S(1)}, f32[1,64]{1,0:T(1,128)}, u32[]{:S(2)}) copy-start(f32[1,64]{1,0:T(1,128)} %get-tuple-element.5) | copy-start | bytes 772

commit v4 on v3

--- a/solution.py
+++ b/solution.py
@@ -28,7 +28,7 @@
 def kernel(
     n_panel, n_dom, scale, images, shift, refs, slots, vol_out, log_out,
     img, refs_in, shift_in, shift_pad, shift_col, refs32, gathered, norms, moved, slot_in, slot_all, onehot,
-    part32, part16, landed, logs, in_sem, recv_sem, z_sem, y_sem, sib_sem, slot_send, slot_recv,
+    part32, part16, landed, logs, in_sem, recv_sem, z_sem, far_sem, y_sem, sib_sem, slot_send, slot_recv,
     part_send, part_recv, log_send, log_recv,
 ):
     n = n_panel * n_dom
@@ -53,6 +53,24 @@
     def place(d):
         return {"panel": lax.div(d, n_dom), "dom": lax.rem(d, n_dom)}
 
+    barrier = pltpu.get_barrier_semaphore()
+
+    @pl.loop(1, n_dom)
+    def _(o):
+        pl.semaphore_signal(
+            barrier, inc=1, device_id={"dom": lax.rem(dom + o, n_dom)}, device_id_type=MESH
+        )
+
+    for step in range(1, n_panel):
+        pl.semaphore_signal(
+            barrier, inc=1, device_id={"panel": lax.rem(panel + step, n_panel)}, device_id_type=MESH
+        )
+
+    for step in range(1, n_y):
+        pl.semaphore_signal(
+            barrier, inc=1, device_id={"panel": y_peer(step), "dom": n_dom - 1 - dom}, device_id_type=MESH
+        )
+
     first = pl.multiple_of(panel * rows, rows)
     refs_copy = pltpu.make_async_copy(refs, refs_in, in_sem.at[0])
     img_copy = pltpu.make_async_copy(images.at[pl.ds(first, rows), :], img, in_sem.at[1])
@@ -63,19 +81,6 @@
     slot_load.start()
     img_copy.start()
 
-    barrier = pltpu.get_barrier_semaphore()
-
-    @pl.loop(1, n_dom)
-    def _(o):
-        pl.semaphore_signal(
-            barrier, inc=1, device_id={"dom": lax.rem(dom + o, n_dom)}, device_id_type=MESH
-        )
-
-    for step in range(1, n_panel):
-        pl.semaphore_signal(
-            barrier, inc=1, device_id={"panel": lax.rem(panel + step, n_panel)}, device_id_type=MESH
-        )
-
     def shard(d):
         return gathered.at[pl.ds(pl.multiple_of(d * TILE, TILE), TILE), :]
 
@@ -95,7 +100,7 @@
     slot_all[panel] = jnp.zeros((segments, LANES), jnp.int32)
     slot_all[panel, :, :slots.shape[1]] = slot_in[...]
 
-    pl.semaphore_wait(barrier, n_dom + n_panel - 2)
+    pl.semaphore_wait(barrier, n_dom + n_panel + n_y - 3)
 
     def shard_copy(d, device, sem):
         return pltpu.make_async_remote_copy(
@@ -106,20 +111,27 @@
     def line_copy(target):
         return shard_copy(me, {"dom": target}, z_sem.at[target])
 
+    def far_copy(step):
+        return shard_copy(me, {"panel": y_peer(step), "dom": n_dom - 1 - dom}, far_sem.at[step - 1])
+
     def y_copy(step, j):
         return shard_copy(panel * n_dom + j, {"panel": y_peer(step)}, y_sem.at[step - 1, j])
 
     def sib_copy(d):
         return shard_copy(d, {"panel": sibling}, sib_sem.at[d])
 
-    def relay(j):
-        for step in range(1, n_y):
-            y_copy(step, j).start()
+    far = n_dom - 1
+    at_end = (dom == 0) | (dom == far)
+
+    def relay(j, across=True):
+        if across:
+            for step in range(1, n_y):
+                y_copy(step, j).start()
         sib_copy(panel * n_dom + j).start()
 
-    def from_line(j):
+    def from_line(j, across):
         sib_copy(panel * n_dom + j).wait_recv()
-        relay(j)
+        relay(j, across)
         add_norm(panel * n_dom + j)
 
     def at_distance(s, do):
@@ -147,9 +159,18 @@
             device_id={"panel": lax.rem(panel + step, n_panel)}, device_id_type=MESH,
         )
 
-    relay(dom)
     for s in range(1, n_dom):
         at_distance(s, lambda target: line_copy(target).start())
+        if s == 1:
+            for step in range(1, n_y):
+                y_copy(step, dom).start()
+
+    @pl.when(at_end)
+    def _():
+        for step in range(1, n_y):
+            far_copy(step).start()
+
+    sib_copy(me).start()
     for step in range(1, n_panel):
         slot_copy(step).start()
 
@@ -242,7 +263,7 @@
         shift_group(t0)
     add_norm(me)
     for s in range(1, n_dom):
-        at_distance(s, from_line)
+        at_distance(s, functools.partial(from_line, across=s < far))
         from_y(s - 1)
         if s == 1:
             build_onehot()
@@ -317,27 +338,33 @@
 
     def part_copy(d):
         return pltpu.make_async_remote_copy(
-            src_ref=tile_of(part16, d), dst_ref=tile_of(landed, me), send_sem=part_send.at[d],
-            recv_sem=part_recv.at[me], device_id=place(d), device_id_type=MESH,
-        )
-
-    def part_landing(d):
-        return pltpu.make_async_remote_copy(
-            src_ref=tile_of(part16, d), dst_ref=tile_of(landed, d), send_sem=part_send.at[d],
-            recv_sem=part_recv.at[d], device_id=place(d), device_id_type=MESH,
-        )
-
-    @pl.loop(1, n)
-    def _(o):
-        part_copy(lax.rem(me + o, n)).start()
-
-    def add_part(o, total):
-        d = lax.rem(me + o, n)
-        part_landing(d).wait_recv()
-        return total + landed[pl.ds(pl.multiple_of(d * TILE, TILE), TILE), :].astype(F32)
-
-    total = part32[pl.ds(pl.multiple_of(me * TILE, TILE), TILE), :]
-    total = lax.fori_loop(1, n, add_part, total) * scale
+            src_ref=tile_of(part16, d), dst_ref=tile_of(landed, me), send_sem=part_send,
+            recv_sem=part_recv, device_id=place(d), device_id_type=MESH,
+        )
+
+    if n <= 16:
+        for far_dom in range(n_dom - 1, -1, -1):
+            for far_panel in range(n_panel):
+                if far_dom or far_panel:
+                    part_copy(
+                        lax.rem(panel + far_panel, n_panel) * n_dom + lax.rem(dom + far_dom, n_dom)
+                    ).start()
+    else:
+        @pl.loop(1, n)
+        def _(o):
+            part_copy(lax.rem(me + o, n)).start()
+
+    own_at = pl.ds(pl.multiple_of(me * TILE, TILE), TILE)
+    landed[own_at, :] = jnp.zeros((TILE, LANES), BF16)
+    arrivals = pltpu.make_async_remote_copy(
+        src_ref=part16.at[:(n - 1) * TILE, :], dst_ref=landed.at[:(n - 1) * TILE, :], send_sem=part_send,
+        recv_sem=part_recv, device_id={"panel": sibling}, device_id_type=MESH,
+    )
+    arrivals.wait_recv()
+    total = part32[own_at, :]
+    for d in range(n):
+        total += landed[d * TILE:(d + 1) * TILE, :].astype(F32)
+    total = total * scale
     for k in range(TILE):
         vol_out[k // lines:k // lines + 1, (k % lines) * LANES:(k % lines + 1) * LANES] = total[k:k + 1]
 
@@ -351,9 +378,12 @@
         log_total += logs[sender]
     log_out[...] = log_total[:1, :log_out.shape[1]]
 
-    @pl.loop(1, n)
-    def _(o):
-        part_copy(lax.rem(me + o, n)).wait_send()
+    arrivals.wait_send()
+
+    @pl.when(at_end)
+    def _():
+        for step in range(1, n_y):
+            far_copy(step).wait_send()
 
     for step in range(1, n_panel):
         slot_copy(step).wait_send()
@@ -363,8 +393,11 @@
         def _():
             line_copy(j).wait_send()
 
-        for step in range(1, n_y):
-            y_copy(step, j).wait_send()
+        @pl.when(jnp.abs(dom - j) != far)
+        def _():
+            for step in range(1, n_y):
+                y_copy(step, j).wait_send()
+
         for step in range(n_y):
             sib_copy(y_peer(step) * n_dom + j).wait_send()
 
@@ -411,12 +444,13 @@
             dma((4,)),
             dma((n,)),
             dma((n_dom,)),
+            dma((max(n_panel // 2 - 1, 1),)),
             dma((max(n_panel // 2 - 1, 1), n_dom)),
             dma((n,)),
             dma((n_panel,)),
             dma((n_panel,)),
-            dma((n,)),
-            dma((n,)),
+            dma(()),
+            dma(()),
             dma((n_panel,)),
             dma((n_panel,)),
         ],

time: 27.7 us -> 28.2 us (1.018)
  Pallas kernels: 25.1 us -> 25.6 us
    pallas_call x1, Pallas kernels: 25.1 us -> 25.6 us  [shards(): pl.pallas_call(functools.partial(kernel, n_panel, n_dom, volume_scale), o...]
where the time goes in v4:
time: 28.2 us; the launch traced here: 28 us
  Pallas kernels  25.6 us (91%)
  local copies, waits for them, and re-layouts  1.81 us (6%)
  between operations  0.65 us (2%)
    pallas_call x1, Pallas kernels, shards(): pl.pallas_call(functools.partial(kernel, n_panel, n_dom, volume_scale), o...  25.6 us
    unnamed x4, local copies, waits for them, and re-layouts  1.81 us

profile of v4, /device:TPU:0, one launch (start us, length us, event | category | flops | bytes accessed | tf_op | source)
XLA Modules:
  0.0 28.0 jit_solution(1866698932966288791)
XLA Ops:
  0.6 25.6 %expectation_backprojection.1 = (f32[2,1024]{1,0:T(2,128)}, f32[1,64]{1,0:T(1,128)}) custom-call(bf16[64,8192]{1,0:T(8,128)(2,1)} %images.1, s32[9,64]{1,0:T(8,128)} %bitcast.3, bf16[4,8192]{1,0:T(4,128)(2,1)} %refs.1, s32[8,16]{1,0:T(8,128)} %bitcast.4), custom_call_target="tpu_custom_call" | custom-call | tf_op jit(solution)/shard_map/expectation_backprojection/pallas_call | solution.py:419
  26.2 0.0 copy-start
  26.2 1.3 %copy.8 = f32[2,1024]{1,0:T(2,128)} copy(f32[2,1024]{1,0:T(2,128)} %get-tuple-element.8) | data formatting | bytes 16384
  27.5 0.0 copy-done
  27.5 0.5 %copy.9 = f32[64]{0:T(128)} copy(f32[64]{0:T(128)S(1)} %bitcast.5) | data formatting | bytes 512
Async XLA Ops:
  26.2 1.3 %copy-start = (f32[1,64]{1,0:T(1,128)S(1)}, f32[1,64]{1,0:T(1,128)}, u32[]{:S(2)}) copy-start(f32[1,64]{1,0:T(1,128)} %get-tuple-element.5) | copy-start | bytes 772

commit v5 on v4

--- a/solution.py
+++ b/solution.py
@@ -28,7 +28,7 @@
 def kernel(
     n_panel, n_dom, scale, images, shift, refs, slots, vol_out, log_out,
     img, refs_in, shift_in, shift_pad, shift_col, refs32, gathered, norms, moved, slot_in, slot_all, onehot,
-    part32, part16, landed, logs, in_sem, recv_sem, z_sem, far_sem, y_sem, sib_sem, slot_send, slot_recv,
+    part32, part16, landed, logs, in_sem, recv_sem, z_sem, y_sem, sib_sem, slot_send, slot_recv,
     part_send, part_recv, log_send, log_recv,
 ):
     n = n_panel * n_dom
@@ -66,11 +66,6 @@
             barrier, inc=1, device_id={"panel": lax.rem(panel + step, n_panel)}, device_id_type=MESH
         )
 
-    for step in range(1, n_y):
-        pl.semaphore_signal(
-            barrier, inc=1, device_id={"panel": y_peer(step), "dom": n_dom - 1 - dom}, device_id_type=MESH
-        )
-
     first = pl.multiple_of(panel * rows, rows)
     refs_copy = pltpu.make_async_copy(refs, refs_in, in_sem.at[0])
     img_copy = pltpu.make_async_copy(images.at[pl.ds(first, rows), :], img, in_sem.at[1])
@@ -100,7 +95,7 @@
     slot_all[panel] = jnp.zeros((segments, LANES), jnp.int32)
     slot_all[panel, :, :slots.shape[1]] = slot_in[...]
 
-    pl.semaphore_wait(barrier, n_dom + n_panel + n_y - 3)
+    pl.semaphore_wait(barrier, n_dom + n_panel - 2)
 
     def shard_copy(d, device, sem):
         return pltpu.make_async_remote_copy(
@@ -111,27 +106,20 @@
     def line_copy(target):
         return shard_copy(me, {"dom": target}, z_sem.at[target])
 
-    def far_copy(step):
-        return shard_copy(me, {"panel": y_peer(step), "dom": n_dom - 1 - dom}, far_sem.at[step - 1])
-
     def y_copy(step, j):
         return shard_copy(panel * n_dom + j, {"panel": y_peer(step)}, y_sem.at[step - 1, j])
 
     def sib_copy(d):
         return shard_copy(d, {"panel": sibling}, sib_sem.at[d])
 
-    far = n_dom - 1
-    at_end = (dom == 0) | (dom == far)
-
-    def relay(j, across=True):
-        if across:
-            for step in range(1, n_y):
-                y_copy(step, j).start()
+    def relay(j):
+        for step in range(1, n_y):
+            y_copy(step, j).start()
         sib_copy(panel * n_dom + j).start()
 
-    def from_line(j, across):
+    def from_line(j):
         sib_copy(panel * n_dom + j).wait_recv()
-        relay(j, across)
+        relay(j)
         add_norm(panel * n_dom + j)
 
     def at_distance(s, do):
@@ -159,17 +147,15 @@
             device_id={"panel": lax.rem(panel + step, n_panel)}, device_id_type=MESH,
         )
 
-    for s in range(1, n_dom):
+    def send_line(s):
         at_distance(s, lambda target: line_copy(target).start())
+
+    late = n_dom - 1 if n_dom > 3 else n_dom
+    for s in range(1, late):
+        send_line(s)
         if s == 1:
             for step in range(1, n_y):
                 y_copy(step, dom).start()
-
-    @pl.when(at_end)
-    def _():
-        for step in range(1, n_y):
-            far_copy(step).start()
-
     sib_copy(me).start()
     for step in range(1, n_panel):
         slot_copy(step).start()
@@ -261,9 +247,11 @@
     img_copy.wait()
     for t0 in range(0, SHIFTS, T_GROUP):
         shift_group(t0)
+    for s in range(late, n_dom):
+        send_line(s)
     add_norm(me)
     for s in range(1, n_dom):
-        at_distance(s, functools.partial(from_line, across=s < far))
+        at_distance(s, from_line)
         from_y(s - 1)
         if s == 1:
             build_onehot()
@@ -380,11 +368,6 @@
 
     arrivals.wait_send()
 
-    @pl.when(at_end)
-    def _():
-        for step in range(1, n_y):
-            far_copy(step).wait_send()
-
     for step in range(1, n_panel):
         slot_copy(step).wait_send()
         log_copy(step).wait_send()
@@ -393,11 +376,8 @@
         def _():
             line_copy(j).wait_send()
 
-        @pl.when(jnp.abs(dom - j) != far)
-        def _():
-            for step in range(1, n_y):
-                y_copy(step, j).wait_send()
-
+        for step in range(1, n_y):
+            y_copy(step, j).wait_send()
         for step in range(n_y):
             sib_copy(y_peer(step) * n_dom + j).wait_send()
 
@@ -444,7 +424,6 @@
             dma((4,)),
             dma((n,)),
             dma((n_dom,)),
-            dma((max(n_panel // 2 - 1, 1),)),
             dma((max(n_panel // 2 - 1, 1), n_dom)),
             dma((n,)),
             dma((n_panel,)),

time: 28.2 us -> 27.4 us (0.972)
  Pallas kernels: 25.6 us -> 24.8 us
    pallas_call x1, Pallas kernels: 25.6 us -> 24.8 us  [shards(): pl.pallas_call(functools.partial(kernel, n_panel, n_dom, volume_scale), o...]
where the time goes in v5:
time: 27.4 us; the launch traced here: 27.3 us
  Pallas kernels  24.8 us (91%)
  local copies, waits for them, and re-layouts  1.81 us (7%)
  between operations  0.65 us (2%)
    pallas_call x1, Pallas kernels, shards(): pl.pallas_call(functools.partial(kernel, n_panel, n_dom, volume_scale), o...  24.8 us
    unnamed x4, local copies, waits for them, and re-layouts  1.81 us

profile of v5, /device:TPU:0, one launch (start us, length us, event | category | flops | bytes accessed | tf_op | source)
XLA Modules:
  0.0 27.3 jit_solution(4884451052910271196)
XLA Ops:
  0.6 24.8 %expectation_backprojection.1 = (f32[2,1024]{1,0:T(2,128)}, f32[1,64]{1,0:T(1,128)}) custom-call(bf16[64,8192]{1,0:T(8,128)(2,1)} %images.1, s32[9,64]{1,0:T(8,128)} %bitcast.3, bf16[4,8192]{1,0:T(4,128)(2,1)} %refs.1, s32[8,16]{1,0:T(8,128)} %bitcast.4), custom_call_target="tpu_custom_call" | custom-call | tf_op jit(solution)/shard_map/expectation_backprojection/pallas_call | solution.py:399
  25.4 0.0 copy-start
  25.4 1.3 %copy.8 = f32[2,1024]{1,0:T(2,128)} copy(f32[2,1024]{1,0:T(2,128)} %get-tuple-element.8) | data formatting | bytes 16384
  26.7 0.0 copy-done
  26.7 0.5 %copy.9 = f32[64]{0:T(128)} copy(f32[64]{0:T(128)S(1)} %bitcast.5) | data formatting | bytes 512
Async XLA Ops:
  25.4 1.3 %copy-start = (f32[1,64]{1,0:T(1,128)S(1)}, f32[1,64]{1,0:T(1,128)}, u32[]{:S(2)}) copy-start(f32[1,64]{1,0:T(1,128)} %get-tuple-element.5) | copy-start | bytes 772

commit v6 on v5

--- a/solution.py
+++ b/solution.py
@@ -434,7 +434,7 @@
             dma((n_panel,)),
         ],
         compiler_params=pltpu.CompilerParams(
-            collective_id=0, has_side_effects=True, vmem_limit_bytes=56 * 1024 * 1024
+            collective_id=0, has_side_effects=True, vmem_limit_bytes=53 * 1024 * 1024
         ),
         name="expectation_backprojection",
     )(images, shift_index.T, references, slot_blocks.T)

time: 27.4 us -> 28.3 us (1.033)
  local copies, waits for them, and re-layouts: 1.81 us -> 3.33 us
  Pallas kernels: 24.8 us -> 24.1 us
    unnamed x4 -> x8, local copies, waits for them, and re-layouts: 1.81 us -> 3.33 us
    pallas_call x1, Pallas kernels: 24.8 us -> 24.1 us  [shards(): pl.pallas_call(functools.partial(kernel, n_panel, n_dom, volume_scale), o...]
where the time goes in v6:
time: 28.3 us; the launch traced here: 28.1 us
  Pallas kernels  24.1 us (85%)
  local copies, waits for them, and re-layouts  3.33 us (12%)
  between operations  0.65 us (2%)
    pallas_call x1, Pallas kernels, shards(): pl.pallas_call(functools.partial(kernel, n_panel, n_dom, volume_scale), o...  24.1 us
    unnamed x8, local copies, waits for them, and re-layouts  3.33 us

profile of v6, /device:TPU:0, one launch (start us, length us, event | category | flops | bytes accessed | tf_op | source)
XLA Modules:
  0.0 28.1 jit_solution(6512864371601935256)
XLA Ops:
  0.6 0.0 copy-start
  0.6 0.8 %copy-done = bf16[4,8192]{1,0:T(4,128)(2,1)S(1)} copy-done((bf16[4,8192]{1,0:T(4,128)(2,1)S(1)}, bf16[4,8192]{1,0:T(4,128)(2,1)}, u32[]{:S(2)}) %copy-start) | copy-done | bytes 65560
  1.5 0.0 copy-start.1
  1.5 0.7 %copy-done.1 = s32[64,9]{0,1:T(8,128)S(1)} copy-done((s32[64,9]{0,1:T(8,128)S(1)}, s32[64,9]{0,1:T(8,128)}, u32[]{:S(2)}) %copy-start.1) | copy-done | bytes 2328
  2.2 0.0 copy-start.2
  2.2 0.7 %copy-done.2 = s32[16,8]{0,1:T(8,128)S(1)} copy-done((s32[16,8]{0,1:T(8,128)S(1)}, s32[16,8]{0,1:T(8,128)}, u32[]{:S(2)}) %copy-start.2) | copy-done | bytes 536
  2.9 24.1 %expectation_backprojection.1 = (f32[2,1024]{1,0:T(2,128)S(1)}, f32[1,64]{1,0:T(1,128)S(1)}) custom-call(bf16[64,8192]{1,0:T(8,128)(2,1)} %images.1, s32[9,64]{1,0:T(8,128)S(1)} %bitcast.3, bf16[4,8192]{1,0:T(4,128)(2,1)S(1)} %copy-done, s32[8,16]{1,0:T(8,128)S(1)} %bitcast.4), custom_call_target="tpu_custom_call" | custom-call | tf_op jit(solution)/shard_map/expectation_backprojection/pallas_call | solution.py:399
  27.0 0.6 %copy.8 = f32[2,1024]{1,0:T(2,128)} copy(f32[2,1024]{1,0:T(2,128)S(1)} %get-tuple-element.8) | data formatting | bytes 16384
  27.6 0.5 %copy.9 = f32[64]{0:T(128)} copy(f32[64]{0:T(128)S(1)} %bitcast.5) | data formatting | bytes 512
Async XLA Ops:
  0.6 0.8 %copy-start = (bf16[4,8192]{1,0:T(4,128)(2,1)S(1)}, bf16[4,8192]{1,0:T(4,128)(2,1)}, u32[]{:S(2)}) copy-start(bf16[4,8192]{1,0:T(4,128)(2,1)} %refs.1) | copy-start | bytes 196612
  1.5 0.7 %copy-start.1 = (s32[64,9]{0,1:T(8,128)S(1)}, s32[64,9]{0,1:T(8,128)}, u32[]{:S(2)}) copy-start(s32[64,9]{0,1:T(8,128)} %param.5) | copy-start | bytes 6916
  2.2 0.7 %copy-start.2 = (s32[16,8]{0,1:T(8,128)S(1)}, s32[16,8]{0,1:T(8,128)}, u32[]{:S(2)}) copy-start(s32[16,8]{0,1:T(8,128)} %param.7) | copy-start | bytes 1540

commit v7 on v5

--- a/solution.py
+++ b/solution.py
@@ -252,12 +252,9 @@
     add_norm(me)
     for s in range(1, n_dom):
         at_distance(s, from_line)
-        from_y(s - 1)
-        if s == 1:
-            build_onehot()
-    if n_dom == 1:
-        build_onehot()
-    from_y(n_dom - 1)
+    build_onehot()
+    for s in range(n_dom):
+        from_y(s)
     for step in range(n_y):
         base = lax.rem(sibling + 2 * step, n_panel) * n_dom
         for j in range(n_dom):

time: 27.4 us -> 27.4 us (level)
  no operation moved by 1% of the time
where the time goes in v7:
time: 27.4 us; the launch traced here: 27.3 us
  Pallas kernels  24.8 us (91%)
  local copies, waits for them, and re-layouts  1.81 us (7%)
  between operations  0.65 us (2%)
    pallas_call x1, Pallas kernels, shards(): pl.pallas_call(functools.partial(kernel, n_panel, n_dom, volume_scale), o...  24.8 us
    unnamed x4, local copies, waits for them, and re-layouts  1.81 us

profile of v7, /device:TPU:0, one launch (start us, length us, event | category | flops | bytes accessed | tf_op | source)
XLA Modules:
  0.0 27.3 jit_solution(12947319089402620359)
XLA Ops:
  0.6 24.8 %expectation_backprojection.1 = (f32[2,1024]{1,0:T(2,128)}, f32[1,64]{1,0:T(1,128)}) custom-call(bf16[64,8192]{1,0:T(8,128)(2,1)} %images.1, s32[9,64]{1,0:T(8,128)} %bitcast.3, bf16[4,8192]{1,0:T(4,128)(2,1)} %refs.1, s32[8,16]{1,0:T(8,128)} %bitcast.4), custom_call_target="tpu_custom_call" | custom-call | tf_op jit(solution)/shard_map/expectation_backprojection/pallas_call | solution.py:396
  25.4 0.0 copy-start
  25.4 1.3 %copy.8 = f32[2,1024]{1,0:T(2,128)} copy(f32[2,1024]{1,0:T(2,128)} %get-tuple-element.8) | data formatting | bytes 16384
  26.7 0.0 copy-done
  26.7 0.5 %copy.9 = f32[64]{0:T(128)} copy(f32[64]{0:T(128)S(1)} %bitcast.5) | data formatting | bytes 512
Async XLA Ops:
  25.4 1.3 %copy-start = (f32[1,64]{1,0:T(1,128)S(1)}, f32[1,64]{1,0:T(1,128)}, u32[]{:S(2)}) copy-start(f32[1,64]{1,0:T(1,128)} %get-tuple-element.5) | copy-start | bytes 772

commit v8 on v7

--- a/solution.py
+++ b/solution.py
@@ -15,6 +15,7 @@
 TILE = 16
 T_GROUP = 3
 U_BLOCK = 8
+HALVES = 2
 PENALTY = 0.125
 F32 = jnp.float32
 BF16 = jnp.bfloat16
@@ -76,8 +77,12 @@
     slot_load.start()
     img_copy.start()
 
-    def shard(d):
-        return gathered.at[pl.ds(pl.multiple_of(d * TILE, TILE), TILE), :]
+    half_width = width // HALVES
+
+    def shard(d, h):
+        return gathered.at[
+            pl.ds(pl.multiple_of(d * TILE, TILE), TILE), h * half_width:(h + 1) * half_width
+        ]
 
     def add_norm(d):
         at = pl.ds(pl.multiple_of(d * TILE, TILE), TILE)
@@ -97,48 +102,63 @@
 
     pl.semaphore_wait(barrier, n_dom + n_panel - 2)
 
-    def shard_copy(d, device, sem):
+    def shard_copy(d, h, device, sem):
         return pltpu.make_async_remote_copy(
-            src_ref=shard(d), dst_ref=shard(d), send_sem=sem, recv_sem=recv_sem.at[d],
+            src_ref=shard(d, h), dst_ref=shard(d, h), send_sem=sem, recv_sem=recv_sem.at[d, h],
             device_id=device, device_id_type=MESH,
         )
 
-    def line_copy(target):
-        return shard_copy(me, {"dom": target}, z_sem.at[target])
-
-    def y_copy(step, j):
-        return shard_copy(panel * n_dom + j, {"panel": y_peer(step)}, y_sem.at[step - 1, j])
-
-    def sib_copy(d):
-        return shard_copy(d, {"panel": sibling}, sib_sem.at[d])
-
-    def relay(j):
-        for step in range(1, n_y):
-            y_copy(step, j).start()
-        sib_copy(panel * n_dom + j).start()
-
-    def from_line(j):
-        sib_copy(panel * n_dom + j).wait_recv()
-        relay(j)
-        add_norm(panel * n_dom + j)
+    def line_copy(target, h):
+        return shard_copy(me, h, {"dom": target}, z_sem.at[target, h])
+
+    def y_copy(step, j, h, cross=0):
+        target = lax.rem(sibling + 2 * step, n_panel) if cross else y_peer(step)
+        return shard_copy(panel * n_dom + j, h, {"panel": target}, y_sem.at[step - 1, j, 2 * h + cross])
+
+    def sib_copy(d, h):
+        return shard_copy(d, h, {"panel": sibling}, sib_sem.at[d, h])
+
+    far = n_dom - 1 if n_dom > 1 else n_dom
 
     def at_distance(s, do):
-        pl.when(dom - s >= 0)(lambda: do(dom - s))
-        pl.when(dom + s < n_dom)(lambda: do(dom + s))
+        for h in range(HALVES):
+            pl.when(dom - s >= 0)(functools.partial(do, dom - s, h))
+            pl.when(dom + s < n_dom)(functools.partial(do, dom + s, h))
+
+    def arrived(d, h):
+        sib_copy(d, h).wait_recv()
+        if h == HALVES - 1:
+            add_norm(d)
+
+    def from_line(s):
+        def pass_on(j, h):
+            sib_copy(panel * n_dom + j, h).wait_recv()
+            for step in range(1, n_y):
+                y_copy(step, j, h).start()
+                if s == far:
+                    y_copy(step, j, h, 1).start()
+            sib_copy(panel * n_dom + j, h).start()
+            if h == HALVES - 1:
+                add_norm(panel * n_dom + j)
+
+        at_distance(s, pass_on)
 
     def from_y(s):
         for step in range(1, n_y):
             base = y_peer(step) * n_dom
 
-            def pass_on(j):
-                sib_copy(base + j).wait_recv()
-                sib_copy(base + j).start()
-                add_norm(base + j)
+            def pass_on(j, h):
+                sib_copy(base + j, h).wait_recv()
+                if s != far:
+                    sib_copy(base + j, h).start()
+                if h == HALVES - 1:
+                    add_norm(base + j)
 
             if s > 0:
                 at_distance(s, pass_on)
             else:
-                pass_on(dom)
+                for h in range(HALVES):
+                    pass_on(dom, h)
 
     def slot_copy(step):
         own = slot_all.at[panel]
@@ -148,15 +168,17 @@
         )
 
     def send_line(s):
-        at_distance(s, lambda target: line_copy(target).start())
+        at_distance(s, lambda target, h: line_copy(target, h).start())
 
     late = n_dom - 1 if n_dom > 3 else n_dom
     for s in range(1, late):
         send_line(s)
         if s == 1:
             for step in range(1, n_y):
-                y_copy(step, dom).start()
-    sib_copy(me).start()
+                for h in range(HALVES):
+                    y_copy(step, dom, h).start()
+    for h in range(HALVES):
+        sib_copy(me, h).start()
     for step in range(1, n_panel):
         slot_copy(step).start()
 
@@ -251,15 +273,15 @@
         send_line(s)
     add_norm(me)
     for s in range(1, n_dom):
-        at_distance(s, from_line)
+        from_line(s)
     build_onehot()
     for s in range(n_dom):
         from_y(s)
     for step in range(n_y):
         base = lax.rem(sibling + 2 * step, n_panel) * n_dom
         for j in range(n_dom):
-            sib_copy(base + j).wait_recv()
-            add_norm(base + j)
+            for h in range(HALVES):
+                arrived(base + j, h)
 
     def fold(q, value):
         return value if q == 0 else pltpu.roll(value, cols - q * ref_rows, 1)
@@ -369,14 +391,14 @@
         slot_copy(step).wait_send()
         log_copy(step).wait_send()
     for j in range(n_dom):
-        @pl.when(j != dom)
-        def _():
-            line_copy(j).wait_send()
-
-        for step in range(1, n_y):
-            y_copy(step, j).wait_send()
-        for step in range(n_y):
-            sib_copy(y_peer(step) * n_dom + j).wait_send()
+        away = jnp.abs(dom - j)
+        for h in range(HALVES):
+            pl.when(away != 0)(lambda: line_copy(j, h).wait_send())
+            sib_copy(panel * n_dom + j, h).wait_send()
+            for step in range(1, n_y):
+                y_copy(step, j, h).wait_send()
+                pl.when(away == far)(lambda: y_copy(step, j, h, 1).wait_send())
+                pl.when(away != far)(lambda: sib_copy(y_peer(step) * n_dom + j, h).wait_send())
 
 
 def shards(images, shift_index, references, slot_blocks):
@@ -419,10 +441,10 @@
             pltpu.VMEM((n * TILE, LANES), BF16),
             pltpu.VMEM((n_panel, 8, LANES), F32),
             dma((4,)),
-            dma((n,)),
-            dma((n_dom,)),
-            dma((max(n_panel // 2 - 1, 1), n_dom)),
-            dma((n,)),
+            dma((n, HALVES)),
+            dma((n_dom, HALVES)),
+            dma((max(n_panel // 2 - 1, 1), n_dom, 2 * HALVES)),
+            dma((n, HALVES)),
             dma((n_panel,)),
             dma((n_panel,)),
             dma(()),

time: 27.4 us -> 27.3 us (level)
  no operation moved by 1% of the time
where the time goes in v8:
time: 27.3 us; the launch traced here: 27.1 us
  Pallas kernels  24.6 us (90%)
  local copies, waits for them, and re-layouts  1.81 us (7%)
  between operations  0.65 us (2%)
    pallas_call x1, Pallas kernels, shards(): pl.pallas_call(functools.partial(kernel, n_panel, n_dom, volume_scale), o...  24.6 us
    unnamed x4, local copies, waits for them, and re-layouts  1.81 us

profile of v8, /device:TPU:0, one launch (start us, length us, event | category | flops | bytes accessed | tf_op | source)
XLA Modules:
  0.0 27.1 jit_solution(824720676365634881)
XLA Ops:
  0.6 24.6 %expectation_backprojection.1 = (f32[2,1024]{1,0:T(2,128)}, f32[1,64]{1,0:T(1,128)}) custom-call(bf16[64,8192]{1,0:T(8,128)(2,1)} %images.1, s32[9,64]{1,0:T(8,128)} %bitcast.3, bf16[4,8192]{1,0:T(4,128)(2,1)} %refs.1, s32[8,16]{1,0:T(8,128)} %bitcast.4), custom_call_target="tpu_custom_call" | custom-call | tf_op jit(solution)/shard_map/expectation_backprojection/pallas_call | solution.py:418
  25.3 0.0 copy-start
  25.3 1.3 %copy.8 = f32[2,1024]{1,0:T(2,128)} copy(f32[2,1024]{1,0:T(2,128)} %get-tuple-element.8) | data formatting | bytes 16384
  26.6 0.0 copy-done
  26.6 0.5 %copy.9 = f32[64]{0:T(128)} copy(f32[64]{0:T(128)S(1)} %bitcast.5) | data formatting | bytes 512
Async XLA Ops:
  25.3 1.3 %copy-start = (f32[1,64]{1,0:T(1,128)S(1)}, f32[1,64]{1,0:T(1,128)}, u32[]{:S(2)}) copy-start(f32[1,64]{1,0:T(1,128)} %get-tuple-element.5) | copy-start | bytes 772

commit v9 on v7

--- a/solution.py
+++ b/solution.py
@@ -87,6 +87,20 @@
             total += value * value
         norms[at, :] = total
 
+    lane = lax.broadcasted_iota(jnp.int32, (rows, LANES), 1)
+    turn_sign = jnp.where(lane < PIX, -1.0, 1.0).astype(F32)
+    freq_col = (lane & (PIX - 1)) - PIX // 2
+
+    shift_copy.wait()
+    shift_pad[...] = jnp.zeros(shift_pad.shape, F32)
+    shift_pad[:SHIFTS, :shift.shape[1]] = shift_in[...].astype(F32)
+    shift_col[...] = jnp.transpose(shift_pad[...]).astype(jnp.int32)
+
+    multiple = lax.broadcasted_iota(jnp.int32, (8, LANES), 0)
+    turns = (freq_col[:8] * multiple + PIX // 2) & (PIX - 1)
+    angle = (turns - PIX // 2).astype(F32) * (-2.0 * math.pi / PIX)
+    cos_rows, sin_rows = jnp.cos(angle), jnp.sin(angle)
+
     refs_copy.wait()
     for q in range(pieces):
         refs32[q * ref_rows:(q + 1) * ref_rows, :] = refs_in[:, q * width:(q + 1) * width].astype(F32)
@@ -159,20 +173,6 @@
     sib_copy(me).start()
     for step in range(1, n_panel):
         slot_copy(step).start()
-
-    lane = lax.broadcasted_iota(jnp.int32, (rows, LANES), 1)
-    turn_sign = jnp.where(lane < PIX, -1.0, 1.0).astype(F32)
-    freq_col = (lane & (PIX - 1)) - PIX // 2
-
-    shift_copy.wait()
-    shift_pad[...] = jnp.zeros(shift_pad.shape, F32)
-    shift_pad[:SHIFTS, :shift.shape[1]] = shift_in[...].astype(F32)
-    shift_col[...] = jnp.transpose(shift_pad[...]).astype(jnp.int32)
-
-    multiple = lax.broadcasted_iota(jnp.int32, (8, LANES), 0)
-    turns = (freq_col[:8] * multiple + PIX // 2) & (PIX - 1)
-    angle = (turns - PIX // 2).astype(F32) * (-2.0 * math.pi / PIX)
-    cos_rows, sin_rows = jnp.cos(angle), jnp.sin(angle)
 
     def offsets(t):
         index = shift_col[pl.ds(first, rows), t:t + 1]
@@ -245,10 +245,11 @@
             ).astype(BF16)
 
     img_copy.wait()
-    for t0 in range(0, SHIFTS, T_GROUP):
-        shift_group(t0)
+    shift_group(0)
     for s in range(late, n_dom):
         send_line(s)
+    for t0 in range(T_GROUP, SHIFTS, T_GROUP):
+        shift_group(t0)
     add_norm(me)
     for s in range(1, n_dom):
         at_distance(s, from_line)

time: 27.4 us -> 27.4 us (level)
  no operation moved by 1% of the time
where the time goes in v9:
time: 27.4 us; the launch traced here: 27.3 us
  Pallas kernels  24.8 us (91%)
  local copies, waits for them, and re-layouts  1.81 us (7%)
  between operations  0.65 us (2%)
    pallas_call x1, Pallas kernels, shards(): pl.pallas_call(functools.partial(kernel, n_panel, n_dom, volume_scale), o...  24.8 us
    unnamed x4, local copies, waits for them, and re-layouts  1.81 us

profile of v9, /device:TPU:0, one launch (start us, length us, event | category | flops | bytes accessed | tf_op | source)
XLA Modules:
  0.0 27.3 jit_solution(17306053641287418298)
XLA Ops:
  0.6 24.8 %expectation_backprojection.1 = (f32[2,1024]{1,0:T(2,128)}, f32[1,64]{1,0:T(1,128)}) custom-call(bf16[64,8192]{1,0:T(8,128)(2,1)} %images.1, s32[9,64]{1,0:T(8,128)} %bitcast.3, bf16[4,8192]{1,0:T(4,128)(2,1)} %refs.1, s32[8,16]{1,0:T(8,128)} %bitcast.4), custom_call_target="tpu_custom_call" | custom-call | tf_op jit(solution)/shard_map/expectation_backprojection/pallas_call | solution.py:397
  25.4 0.0 copy-start
  25.4 1.3 %copy.8 = f32[2,1024]{1,0:T(2,128)} copy(f32[2,1024]{1,0:T(2,128)} %get-tuple-element.8) | data formatting | bytes 16384
  26.7 0.0 copy-done
  26.7 0.5 %copy.9 = f32[64]{0:T(128)} copy(f32[64]{0:T(128)S(1)} %bitcast.5) | data formatting | bytes 512
Async XLA Ops:
  25.4 1.3 %copy-start = (f32[1,64]{1,0:T(1,128)S(1)}, f32[1,64]{1,0:T(1,128)}, u32[]{:S(2)}) copy-start(f32[1,64]{1,0:T(1,128)} %get-tuple-element.5) | copy-start | bytes 772
